TPU v7x, 32 devices: a whole 2x2x4 slice. The times are simulated.
32 devices in a mesh: pipe: 2 (over core), seq: 4 (over y, x), batch: 4 (over z).
Axes of the slice: x: 2, y: 2, z: 4, core: 2. Of those that a mesh axis runs over, the one named last changes fastest.
Arguments:
- latent: bfloat16 [32, 32, 2560], P('batch', 'seq'), parts along dimension 0, may hold values from -6 to 6
- w_qkv: bfloat16 [2, 2560, 3, 2560], P('pipe', None, None, 'seq')
- modulation: float32 [2, 8, 3, 2560], P('pipe'), may hold values from -3 to 3
- timestep: int32 [1], replicated, may hold values from 0 to 7
- order: int32 [32], P('batch'), parts along dimension 0, may hold values from 0 to 7, each once
- tiles: int32 [64, 6], P('batch'), parts along dimension 0, may hold values from 0 to 15, as said below
- stale_kv: bfloat16 [2, 32, 32, 2, 2560], P('pipe', 'batch', None, None, 'seq'), parts along dimension 1, may hold values from -6 to 6
Outputs:
- section_out: bfloat16 [2, 32, 32, 2560], P('pipe', 'batch', 'seq'), parts along dimension 1
There are 4 independent parts, one for each index of `batch`. A program takes and returns all parts, laid end to end along the dimension named above; an argument that names none is the same for every part. Nothing has to cross between parts.
Inputs may be any that keep to these rules, and one draw needn't show every extreme that they name: Row g lists tile g first, then 6 - 1 distinct other tiles whose index differs from g modulo 16 by 1 to 5.
All inputs are finite; a program needn't handle non-finite values.
Results may differ from a plain program's by a relative error of at most 0.019.
Values may be sent and summed in bfloat16 or wider, within the bound.
A program may use at most 128 MiB of HBM per device.

v0:
```python
import jax
import jax.numpy as jnp
from jax import lax
from jax.sharding import PartitionSpec as P

HEAD_DIM = 128
TILES_P = 2


epsilon = 1e-06


def shifted(value, axis, by):
    count = lax.axis_size(axis)
    pairs = [(i, i + by) for i in range(count) if 0 <= i + by < count]
    return lax.ppermute(value, axis, pairs)


def normalize(row_block, shift_row, scale_row):
    floated = row_block.astype(jnp.float32)
    average = jnp.mean(floated, axis=-1, keepdims=True)
    centred = floated - average
    spread = jnp.mean(centred * centred, axis=-1, keepdims=True)
    return (centred * lax.rsqrt(spread + epsilon) * (1.0 + scale_row) + shift_row).astype(
        jnp.bfloat16
    )


def attend(query, buffer, chosen_tiles, heads_local, tile_len):
    patches, patch_tok, kv_pair, local_w = buffer.shape
    tiles_patch, chosen_count = chosen_tiles.shape
    head_width = local_w // heads_local
    blocks = buffer.reshape(patches * patch_tok // tile_len, tile_len, kv_pair, local_w)
    picked = blocks[chosen_tiles].reshape(
        tiles_patch, chosen_count * tile_len, kv_pair, heads_local, head_width
    )
    queries = query.reshape(tiles_patch, tile_len, heads_local, head_width)
    scores = jnp.einsum(
        "qthd,qkhd->qhtk", queries, picked[:, :, 0], preferred_element_type=jnp.float32
    )
    scores = scores * head_width ** (-0.5)
    largest = jnp.max(scores, axis=-1, keepdims=True)
    raised = jnp.exp(scores - largest)
    probabilities = (raised / jnp.sum(raised, axis=-1, keepdims=True)).astype(jnp.bfloat16)
    mixed = jnp.einsum(
        "qhtk,qkhd->qthd", probabilities, picked[:, :, 1], preferred_element_type=jnp.float32
    )
    return mixed.reshape(tiles_patch * tile_len, local_w).astype(jnp.bfloat16)


def pass_on(updated):
    return shifted(updated, "pipe", 1)


def local(latent, w_qkv, modulation, timestep, order, tiles, stale_kv):
    patches, rows_dev, width = latent.shape
    local_w = w_qkv.shape[3]
    heads_local = local_w // HEAD_DIM
    seq_count = lax.axis_size("seq")
    pipe_count = lax.axis_size("pipe")
    section_rank = lax.axis_index("pipe")
    seq_rank = lax.axis_index("seq")
    patch_tok = rows_dev * seq_count
    tiles_patch = TILES_P
    tile_len = patch_tok // tiles_patch
    weights = w_qkv[0].reshape(width, 3 * local_w)
    mod_row = lax.dynamic_index_in_dim(modulation[0], timestep[0], 0, keepdims=False)
    shift_row = mod_row[0]
    scale_row = mod_row[1]
    gate_row = mod_row[2]
    gate_local = lax.dynamic_slice_in_dim(gate_row, seq_rank * local_w, local_w)
    tick_count = patches + pipe_count - 1

    def project(row_block):
        normed = normalize(row_block, shift_row, scale_row)
        projected = jnp.dot(normed, weights, preferred_element_type=jnp.float32).astype(
            jnp.bfloat16
        )
        return projected.reshape(row_block.shape[0], 3, local_w)

    def common(tick):
        position = tick - section_rank
        active = (position >= 0) & (position < patches)
        patch_id = order[jnp.clip(position, 0, patches - 1)]
        return (active, patch_id)

    def attend_patch(projected, buffer, active, patch_id):
        previous = lax.dynamic_index_in_dim(buffer, patch_id, 0, keepdims=False)
        fresh_kv = jnp.where(active, projected[:, 1:], previous)
        buffer = lax.dynamic_update_index_in_dim(buffer, fresh_kv, patch_id, 0)
        chosen = lax.dynamic_slice_in_dim(tiles, patch_id * tiles_patch, tiles_patch, 0)
        return (attend(projected[:, 0], buffer, chosen, heads_local, tile_len), buffer)

    def record(results, updated, active, patch_id):
        previous = lax.dynamic_index_in_dim(results, patch_id, 0, keepdims=False)
        kept = jnp.where(active, updated, previous)
        return lax.dynamic_update_index_in_dim(results, kept, patch_id, 0)

    columns_in = lax.all_to_all(latent, "seq", split_axis=2, concat_axis=1, tiled=True)

    def tick_columns(carry, tick):
        incoming, buffer, results = carry
        active, patch_id = common(tick)
        own_rows = jnp.where(
            section_rank == 0,
            lax.dynamic_index_in_dim(columns_in, patch_id, 0, keepdims=False),
            incoming,
        )
        gathered = lax.all_gather(own_rows, "seq", axis=1, tiled=True)
        projected = project(gathered)
        attended, buffer = attend_patch(projected, buffer, active, patch_id)
        updated = (own_rows.astype(jnp.float32) + gate_local * attended.astype(jnp.float32)).astype(
            jnp.bfloat16
        )
        results = record(results, updated, active, patch_id)
        return ((pass_on(updated), buffer, results), None)

    start_carry = (
        jnp.zeros((patch_tok, local_w), jnp.bfloat16),
        stale_kv[0],
        jnp.zeros_like(columns_in),
    )
    final_carry, unused = lax.scan(
        tick_columns, start_carry, jnp.arange(tick_count, dtype=jnp.int32)
    )
    finished = lax.all_to_all(final_carry[2], "seq", split_axis=1, concat_axis=2, tiled=True)
    return finished[None]


def solution(mesh):
    return jax.shard_map(
        local,
        mesh=mesh,
        in_specs=(
            P("batch", "seq", None),
            P("pipe", None, None, "seq"),
            P("pipe", None, None, None),
            P(),
            P("batch"),
            P("batch", None),
            P("pipe", "batch", None, None, "seq"),
        ),
        out_specs=P("pipe", "batch", "seq", None),
        check_vma=False,
    )
```

profile of v0, /device:TPU:1, one launch (start us, length us, event | category | flops | bytes accessed | tf_op | source)
XLA Modules:
  0.0 286.4 jit_solution(8915465724319887964)
XLA Ops:
  0.0 5.5 %copy.46 = bf16[8,8,2560]{1,0,2:T(8,128)(2,1)} copy(bf16[8,8,2560]{2,1,0:T(8,128)(2,1)} %param.9) | data formatting | bytes 655360 | tf_op args[0]
  5.5 7.5 %reshape.63 = bf16[4,2,20480]{2,1,0:T(2,128)(2,1)} reshape(bf16[2560,8,8]{2,1,0:T(8,128)(2,1)} %bitcast.93) | data formatting | bytes 655360
  13.0 4.3 %all-to-all-start = ((bf16[4,2,20480]{2,1,0:T(2,128)(2,1)}), bf16[4,2,20480]{2,1,0:T(2,128)(2,1)S(1)}, u32[]{:S(2)}, u32[]{:S(2)}) async-start(bf16[4,2,20480]{2,1,0:T(2,128)(2,1)} %reshape.63), calls=%async_computation | async-start | bytes 655360 | tf_op jit(solution)/shard_map/all_to_all | solution.py:99
  17.9 13.8 %copy.48 = bf16[1,2560,3,640]{1,3,2,0:T(8,128)(2,1)} copy(bf16[1,2560,3,640]{3,1,2,0:T(8,128)(2,1)} %param.10) | data formatting | bytes 19660800 | tf_op args[1]
  31.8 14.5 %copy.49 = bf16[2560,1920]{1,0:T(8,128)(2,1)} copy(bf16[2560,1920]{0,1:T(8,128)(2,1)} %bitcast.89) | data formatting | bytes 19660800 | tf_op jit(solution)/shard_map/while | solution.py:123
  48.2 7.2 %reshape.64 = bf16[2560,8,8]{2,1,0:T(8,128)(2,1)} reshape(bf16[4,2,20480]{2,1,0:T(2,128)(2,1)S(1)} %all-to-all-done) | data formatting | bytes 655360
  55.4 4.8 %copy.47 = bf16[8,4,8,640]{3,2,1,0:T(8,128)(2,1)S(1)} copy(bf16[8,4,8,640]{2,0,3,1:T(8,128)(2,1)} %bitcast.92) | data formatting | bytes 655360 | tf_op jit(solution)/shard_map/all_to_all | solution.py:99
  60.3 217.0 %while.15 = (s32[]{:T(128)}, bf16[32,640]{1,0:T(8,128)(2,1)S(1)}, bf16[8,32,2,640]{3,1,0,2:T(8,128)(2,1)S(1)}, bf16[8,32,640]{2,1,0:T(8,128)(2,1)S(1)}, pred[]{:...) while((s32[]{:T(128)}, bf16[32,640]{1,0:T(8,128)(2,1)S(1)}, ...), condition=%wide.region_5.6_spmd, body=%wide.region_0.5_spmd.sunk | while | flops 323782560 | bytes 18574404 | solution.py:123
  64.1 7.3 %all_gather.5 = bf16[32,2560]{1,0:T(8,128)(2,1)S(1)} all-gather(bf16[32,640]{1,0:T(8,128)(2,1)S(1)} %bitcast_select_fusion.3), channel_id=1, replica_groups=mesh['pipe'=2,'seq'=4,'batch'=4] {'seq'}, dimensions={1}, use_global_device_ids=true | all-gather | bytes 204800 | tf_op jit(solution)/shard_map/while/body/eval_jaxpr/all_gather | solution.py:109
  71.9 5.6 %convolution_convert_fusion.3 = bf16[32,1920]{1,0:T(8,128)(2,1)S(1)} fusion(bf16[2560,1920]{1,0:T(8,128)(2,1)} %get-tuple-element.381, bf16[32,2560]{1,0:T(8,128)(2,1)S(1)} %all_gather.5, f32[2560]{0:T(1024)S(1)} %reduce.10, f32[2560]{0:T(1024)S(1)} %broadcast_add_fusion.2, f32[32]{0:T(128)S(1)} %add_rsqrt_fusion.2, f32[32]{0:T(128)S(1)} %broadcast_multiply_fusion.2), kind=kOutput, calls=%fused_computation.2.clone.1 | convolution fusion | flops 315125760 | bytes 10137856 | tf_op jit(solution)/shard_map/while/body/eval_jaxpr/dot_general | solution.py:76
  82.5 3.6 %collective-permute-done = bf16[32,640]{1,0:T(8,128)(2,1)S(1)} collective-permute-done((bf16[32,640]{1,0:T(8,128)(2,1)S(1)}, bf16[32,640]{1,0:T(8,128)(2,1)S(1)}, u32[]{:S(2)}, u32[]{:S(2)}) %collective-permute-start) | collective-permute-done | bytes 40992 | tf_op jit(solution)/shard_map/while/body/eval_jaxpr/ppermute | solution.py:16
  89.8 6.8 %all_gather.5 = bf16[32,2560]{1,0:T(8,128)(2,1)S(1)} all-gather(bf16[32,640]{1,0:T(8,128)(2,1)S(1)} %bitcast_select_fusion.3), channel_id=1, replica_groups=mesh['pipe'=2,'seq'=4,'batch'=4] {'seq'}, dimensions={1}, use_global_device_ids=true | all-gather | bytes 204800 | tf_op jit(solution)/shard_map/while/body/eval_jaxpr/all_gather | solution.py:109
  97.1 5.6 %convolution_convert_fusion.3 = bf16[32,1920]{1,0:T(8,128)(2,1)S(1)} fusion(bf16[2560,1920]{1,0:T(8,128)(2,1)} %get-tuple-element.381, bf16[32,2560]{1,0:T(8,128)(2,1)S(1)} %all_gather.5, f32[2560]{0:T(1024)S(1)} %reduce.10, f32[2560]{0:T(1024)S(1)} %broadcast_add_fusion.2, f32[32]{0:T(128)S(1)} %add_rsqrt_fusion.2, f32[32]{0:T(128)S(1)} %broadcast_multiply_fusion.2), kind=kOutput, calls=%fused_computation.2.clone.1 | convolution fusion | flops 315125760 | bytes 10137856 | tf_op jit(solution)/shard_map/while/body/eval_jaxpr/dot_general | solution.py:76
  107.7 2.9 %collective-permute-done = bf16[32,640]{1,0:T(8,128)(2,1)S(1)} collective-permute-done((bf16[32,640]{1,0:T(8,128)(2,1)S(1)}, bf16[32,640]{1,0:T(8,128)(2,1)S(1)}, u32[]{:S(2)}, u32[]{:S(2)}) %collective-permute-start) | collective-permute-done | bytes 40992 | tf_op jit(solution)/shard_map/while/body/eval_jaxpr/ppermute | solution.py:16
  114.4 5.6 %all_gather.5 = bf16[32,2560]{1,0:T(8,128)(2,1)S(1)} all-gather(bf16[32,640]{1,0:T(8,128)(2,1)S(1)} %bitcast_select_fusion.3), channel_id=1, replica_groups=mesh['pipe'=2,'seq'=4,'batch'=4] {'seq'}, dimensions={1}, use_global_device_ids=true | all-gather | bytes 204800 | tf_op jit(solution)/shard_map/while/body/eval_jaxpr/all_gather | solution.py:109
  120.4 5.6 %convolution_convert_fusion.3 = bf16[32,1920]{1,0:T(8,128)(2,1)S(1)} fusion(bf16[2560,1920]{1,0:T(8,128)(2,1)} %get-tuple-element.381, bf16[32,2560]{1,0:T(8,128)(2,1)S(1)} %all_gather.5, f32[2560]{0:T(1024)S(1)} %reduce.10, f32[2560]{0:T(1024)S(1)} %broadcast_add_fusion.2, f32[32]{0:T(128)S(1)} %add_rsqrt_fusion.2, f32[32]{0:T(128)S(1)} %broadcast_multiply_fusion.2), kind=kOutput, calls=%fused_computation.2.clone.1 | convolution fusion | flops 315125760 | bytes 10137856 | tf_op jit(solution)/shard_map/while/body/eval_jaxpr/dot_general | solution.py:76
  131.0 2.9 %collective-permute-done = bf16[32,640]{1,0:T(8,128)(2,1)S(1)} collective-permute-done((bf16[32,640]{1,0:T(8,128)(2,1)S(1)}, bf16[32,640]{1,0:T(8,128)(2,1)S(1)}, u32[]{:S(2)}, u32[]{:S(2)}) %collective-permute-start) | collective-permute-done | bytes 40992 | tf_op jit(solution)/shard_map/while/body/eval_jaxpr/ppermute | solution.py:16
  137.7 6.8 %all_gather.5 = bf16[32,2560]{1,0:T(8,128)(2,1)S(1)} all-gather(bf16[32,640]{1,0:T(8,128)(2,1)S(1)} %bitcast_select_fusion.3), channel_id=1, replica_groups=mesh['pipe'=2,'seq'=4,'batch'=4] {'seq'}, dimensions={1}, use_global_device_ids=true | all-gather | bytes 204800 | tf_op jit(solution)/shard_map/while/body/eval_jaxpr/all_gather | solution.py:109
  144.9 5.6 %convolution_convert_fusion.3 = bf16[32,1920]{1,0:T(8,128)(2,1)S(1)} fusion(bf16[2560,1920]{1,0:T(8,128)(2,1)} %get-tuple-element.381, bf16[32,2560]{1,0:T(8,128)(2,1)S(1)} %all_gather.5, f32[2560]{0:T(1024)S(1)} %reduce.10, f32[2560]{0:T(1024)S(1)} %broadcast_add_fusion.2, f32[32]{0:T(128)S(1)} %add_rsqrt_fusion.2, f32[32]{0:T(128)S(1)} %broadcast_multiply_fusion.2), kind=kOutput, calls=%fused_computation.2.clone.1 | convolution fusion | flops 315125760 | bytes 10137856 | tf_op jit(solution)/shard_map/while/body/eval_jaxpr/dot_general | solution.py:76
  162.2 5.6 %all_gather.5 = bf16[32,2560]{1,0:T(8,128)(2,1)S(1)} all-gather(bf16[32,640]{1,0:T(8,128)(2,1)S(1)} %bitcast_select_fusion.3), channel_id=1, replica_groups=mesh['pipe'=2,'seq'=4,'batch'=4] {'seq'}, dimensions={1}, use_global_device_ids=true | all-gather | bytes 204800 | tf_op jit(solution)/shard_map/while/body/eval_jaxpr/all_gather | solution.py:109
  168.2 5.6 %convolution_convert_fusion.3 = bf16[32,1920]{1,0:T(8,128)(2,1)S(1)} fusion(bf16[2560,1920]{1,0:T(8,128)(2,1)} %get-tuple-element.381, bf16[32,2560]{1,0:T(8,128)(2,1)S(1)} %all_gather.5, f32[2560]{0:T(1024)S(1)} %reduce.10, f32[2560]{0:T(1024)S(1)} %broadcast_add_fusion.2, f32[32]{0:T(128)S(1)} %add_rsqrt_fusion.2, f32[32]{0:T(128)S(1)} %broadcast_multiply_fusion.2), kind=kOutput, calls=%fused_computation.2.clone.1 | convolution fusion | flops 315125760 | bytes 10137856 | tf_op jit(solution)/shard_map/while/body/eval_jaxpr/dot_general | solution.py:76
  185.5 6.8 %all_gather.5 = bf16[32,2560]{1,0:T(8,128)(2,1)S(1)} all-gather(bf16[32,640]{1,0:T(8,128)(2,1)S(1)} %bitcast_select_fusion.3), channel_id=1, replica_groups=mesh['pipe'=2,'seq'=4,'batch'=4] {'seq'}, dimensions={1}, use_global_device_ids=true | all-gather | bytes 204800 | tf_op jit(solution)/shard_map/while/body/eval_jaxpr/all_gather | solution.py:109
  192.7 5.6 %convolution_convert_fusion.3 = bf16[32,1920]{1,0:T(8,128)(2,1)S(1)} fusion(bf16[2560,1920]{1,0:T(8,128)(2,1)} %get-tuple-element.381, bf16[32,2560]{1,0:T(8,128)(2,1)S(1)} %all_gather.5, f32[2560]{0:T(1024)S(1)} %reduce.10, f32[2560]{0:T(1024)S(1)} %broadcast_add_fusion.2, f32[32]{0:T(128)S(1)} %add_rsqrt_fusion.2, f32[32]{0:T(128)S(1)} %broadcast_multiply_fusion.2), kind=kOutput, calls=%fused_computation.2.clone.1 | convolution fusion | flops 315125760 | bytes 10137856 | tf_op jit(solution)/shard_map/while/body/eval_jaxpr/dot_general | solution.py:76
  210.0 5.6 %all_gather.5 = bf16[32,2560]{1,0:T(8,128)(2,1)S(1)} all-gather(bf16[32,640]{1,0:T(8,128)(2,1)S(1)} %bitcast_select_fusion.3), channel_id=1, replica_groups=mesh['pipe'=2,'seq'=4,'batch'=4] {'seq'}, dimensions={1}, use_global_device_ids=true | all-gather | bytes 204800 | tf_op jit(solution)/shard_map/while/body/eval_jaxpr/all_gather | solution.py:109
  216.0 5.6 %convolution_convert_fusion.3 = bf16[32,1920]{1,0:T(8,128)(2,1)S(1)} fusion(bf16[2560,1920]{1,0:T(8,128)(2,1)} %get-tuple-element.381, bf16[32,2560]{1,0:T(8,128)(2,1)S(1)} %all_gather.5, f32[2560]{0:T(1024)S(1)} %reduce.10, f32[2560]{0:T(1024)S(1)} %broadcast_add_fusion.2, f32[32]{0:T(128)S(1)} %add_rsqrt_fusion.2, f32[32]{0:T(128)S(1)} %broadcast_multiply_fusion.2), kind=kOutput, calls=%fused_computation.2.clone.1 | convolution fusion | flops 315125760 | bytes 10137856 | tf_op jit(solution)/shard_map/while/body/eval_jaxpr/dot_general | solution.py:76
  226.6 2.9 %collective-permute-done = bf16[32,640]{1,0:T(8,128)(2,1)S(1)} collective-permute-done((bf16[32,640]{1,0:T(8,128)(2,1)S(1)}, bf16[32,640]{1,0:T(8,128)(2,1)S(1)}, u32[]{:S(2)}, u32[]{:S(2)}) %collective-permute-start) | collective-permute-done | bytes 40992 | tf_op jit(solution)/shard_map/while/body/eval_jaxpr/ppermute | solution.py:16
  233.3 6.8 %all_gather.5 = bf16[32,2560]{1,0:T(8,128)(2,1)S(1)} all-gather(bf16[32,640]{1,0:T(8,128)(2,1)S(1)} %bitcast_select_fusion.3), channel_id=1, replica_groups=mesh['pipe'=2,'seq'=4,'batch'=4] {'seq'}, dimensions={1}, use_global_device_ids=true | all-gather | bytes 204800 | tf_op jit(solution)/shard_map/while/body/eval_jaxpr/all_gather | solution.py:109
  240.5 5.6 %convolution_convert_fusion.3 = bf16[32,1920]{1,0:T(8,128)(2,1)S(1)} fusion(bf16[2560,1920]{1,0:T(8,128)(2,1)} %get-tuple-element.381, bf16[32,2560]{1,0:T(8,128)(2,1)S(1)} %all_gather.5, f32[2560]{0:T(1024)S(1)} %reduce.10, f32[2560]{0:T(1024)S(1)} %broadcast_add_fusion.2, f32[32]{0:T(128)S(1)} %add_rsqrt_fusion.2, f32[32]{0:T(128)S(1)} %broadcast_multiply_fusion.2), kind=kOutput, calls=%fused_computation.2.clone.1 | convolution fusion | flops 315125760 | bytes 10137856 | tf_op jit(solution)/shard_map/while/body/eval_jaxpr/dot_general | solution.py:76
  251.2 2.9 %collective-permute-done = bf16[32,640]{1,0:T(8,128)(2,1)S(1)} collective-permute-done((bf16[32,640]{1,0:T(8,128)(2,1)S(1)}, bf16[32,640]{1,0:T(8,128)(2,1)S(1)}, u32[]{:S(2)}, u32[]{:S(2)}) %collective-permute-start) | collective-permute-done | bytes 40992 | tf_op jit(solution)/shard_map/while/body/eval_jaxpr/ppermute | solution.py:16
  257.8 5.6 %all_gather.5 = bf16[32,2560]{1,0:T(8,128)(2,1)S(1)} all-gather(bf16[32,640]{1,0:T(8,128)(2,1)S(1)} %bitcast_select_fusion.3), channel_id=1, replica_groups=mesh['pipe'=2,'seq'=4,'batch'=4] {'seq'}, dimensions={1}, use_global_device_ids=true | all-gather | bytes 204800 | tf_op jit(solution)/shard_map/while/body/eval_jaxpr/all_gather | solution.py:109
  263.8 5.6 %convolution_convert_fusion.3 = bf16[32,1920]{1,0:T(8,128)(2,1)S(1)} fusion(bf16[2560,1920]{1,0:T(8,128)(2,1)} %get-tuple-element.381, bf16[32,2560]{1,0:T(8,128)(2,1)S(1)} %all_gather.5, f32[2560]{0:T(1024)S(1)} %reduce.10, f32[2560]{0:T(1024)S(1)} %broadcast_add_fusion.2, f32[32]{0:T(128)S(1)} %add_rsqrt_fusion.2, f32[32]{0:T(128)S(1)} %broadcast_multiply_fusion.2), kind=kOutput, calls=%fused_computation.2.clone.1 | convolution fusion | flops 315125760 | bytes 10137856 | tf_op jit(solution)/shard_map/while/body/eval_jaxpr/dot_general | solution.py:76
  277.4 8.2 %all_to_all.33 = bf16[8,32,640]{2,0,1:T(8,128)(2,1)S(1)} all-to-all(bf16[8,32,640]{2,0,1:T(8,128)(2,1)S(1)} %copy.51), channel_id=1, replica_groups=mesh['pipe'=2,'seq'=4,'batch'=4] {'seq'}, dimensions={1} | all-to-all | bytes 655360 | tf_op jit(solution)/shard_map/all_to_all | solution.py:126
  (290 shorter events, 66.7 us)
Async XLA Ops:
  13.0 35.2 %all-to-all-start = ((bf16[4,2,20480]{2,1,0:T(2,128)(2,1)}), bf16[4,2,20480]{2,1,0:T(2,128)(2,1)S(1)}, u32[]{:S(2)}, u32[]{:S(2)}) async-start(bf16[4,2,20480]{2,1,0:T(2,128)(2,1)} %reshape.63), calls=%async_computation | async-start | bytes 655360 | tf_op jit(solution)/shard_map/all_to_all | solution.py:99
  31.8 14.5 %copy-start = (bf16[1,8,32,2,640]{4,3,2,1,0:T(2,128)(2,1)S(1)}, bf16[1,8,32,2,640]{4,3,2,1,0:T(2,128)(2,1)}, u32[]{:S(2)}) copy-start(bf16[1,8,32,2,640]{4,3,2,1,0:T(2,128)(2,1)} %param.15) | copy-start | bytes 1966084
  31.8 14.6 %copy-start.1 = (s32[16,6]{0,1:T(8,128)S(1)}, s32[16,6]{0,1:T(8,128)}, u32[]{:S(2)}) copy-start(s32[16,6]{0,1:T(8,128)} %param.14) | copy-start | bytes 1156
  46.2 14.1 %copy-start.2 = (s32[8]{0:T(128)S(1)}, s32[8]{0:T(128)}, u32[]{:S(2)}) copy-start(s32[8]{0:T(128)} %param.13) | copy-start | bytes 100
  81.2 4.9 %collective-permute-start = (bf16[32,640]{1,0:T(8,128)(2,1)S(1)}, bf16[32,640]{1,0:T(8,128)(2,1)S(1)}, u32[]{:S(2)}, u32[]{:S(2)}) collective-permute-start(bf16[32,640]{1,0:T(8,128)(2,1)S(1)} %get-tuple-element.325), channel_id=1, source_target_pairs={{0,16},{1,17},{2,18},{3,19},{4,20},{5,21},{6,22},{7,23},{8,24},{9,... | collective-permute-start | bytes 122888 | tf_op jit(solution)/shard_map/while/body/eval_jaxpr/ppermute | solution.py:16
  106.4 4.2 %collective-permute-start = (bf16[32,640]{1,0:T(8,128)(2,1)S(1)}, bf16[32,640]{1,0:T(8,128)(2,1)S(1)}, u32[]{:S(2)}, u32[]{:S(2)}) collective-permute-start(bf16[32,640]{1,0:T(8,128)(2,1)S(1)} %get-tuple-element.325), channel_id=1, source_target_pairs={{0,16},{1,17},{2,18},{3,19},{4,20},{5,21},{6,22},{7,23},{8,24},{9,... | collective-permute-start | bytes 122888 | tf_op jit(solution)/shard_map/while/body/eval_jaxpr/ppermute | solution.py:16
  129.7 4.2 %collective-permute-start = (bf16[32,640]{1,0:T(8,128)(2,1)S(1)}, bf16[32,640]{1,0:T(8,128)(2,1)S(1)}, u32[]{:S(2)}, u32[]{:S(2)}) collective-permute-start(bf16[32,640]{1,0:T(8,128)(2,1)S(1)} %get-tuple-element.325), channel_id=1, source_target_pairs={{0,16},{1,17},{2,18},{3,19},{4,20},{5,21},{6,22},{7,23},{8,24},{9,... | collective-permute-start | bytes 122888 | tf_op jit(solution)/shard_map/while/body/eval_jaxpr/ppermute | solution.py:16
  154.2 4.2 %collective-permute-start = (bf16[32,640]{1,0:T(8,128)(2,1)S(1)}, bf16[32,640]{1,0:T(8,128)(2,1)S(1)}, u32[]{:S(2)}, u32[]{:S(2)}) collective-permute-start(bf16[32,640]{1,0:T(8,128)(2,1)S(1)} %get-tuple-element.325), channel_id=1, source_target_pairs={{0,16},{1,17},{2,18},{3,19},{4,20},{5,21},{6,22},{7,23},{8,24},{9,... | collective-permute-start | bytes 122888 | tf_op jit(solution)/shard_map/while/body/eval_jaxpr/ppermute | solution.py:16
  177.5 4.2 %collective-permute-start = (bf16[32,640]{1,0:T(8,128)(2,1)S(1)}, bf16[32,640]{1,0:T(8,128)(2,1)S(1)}, u32[]{:S(2)}, u32[]{:S(2)}) collective-permute-start(bf16[32,640]{1,0:T(8,128)(2,1)S(1)} %get-tuple-element.325), channel_id=1, source_target_pairs={{0,16},{1,17},{2,18},{3,19},{4,20},{5,21},{6,22},{7,23},{8,24},{9,... | collective-permute-start | bytes 122888 | tf_op jit(solution)/shard_map/while/body/eval_jaxpr/ppermute | solution.py:16
  202.0 4.2 %collective-permute-start = (bf16[32,640]{1,0:T(8,128)(2,1)S(1)}, bf16[32,640]{1,0:T(8,128)(2,1)S(1)}, u32[]{:S(2)}, u32[]{:S(2)}) collective-permute-start(bf16[32,640]{1,0:T(8,128)(2,1)S(1)} %get-tuple-element.325), channel_id=1, source_target_pairs={{0,16},{1,17},{2,18},{3,19},{4,20},{5,21},{6,22},{7,23},{8,24},{9,... | collective-permute-start | bytes 122888 | tf_op jit(solution)/shard_map/while/body/eval_jaxpr/ppermute | solution.py:16
  225.3 4.2 %collective-permute-start = (bf16[32,640]{1,0:T(8,128)(2,1)S(1)}, bf16[32,640]{1,0:T(8,128)(2,1)S(1)}, u32[]{:S(2)}, u32[]{:S(2)}) collective-permute-start(bf16[32,640]{1,0:T(8,128)(2,1)S(1)} %get-tuple-element.325), channel_id=1, source_target_pairs={{0,16},{1,17},{2,18},{3,19},{4,20},{5,21},{6,22},{7,23},{8,24},{9,... | collective-permute-start | bytes 122888 | tf_op jit(solution)/shard_map/while/body/eval_jaxpr/ppermute | solution.py:16
  249.9 4.2 %collective-permute-start = (bf16[32,640]{1,0:T(8,128)(2,1)S(1)}, bf16[32,640]{1,0:T(8,128)(2,1)S(1)}, u32[]{:S(2)}, u32[]{:S(2)}) collective-permute-start(bf16[32,640]{1,0:T(8,128)(2,1)S(1)} %get-tuple-element.325), channel_id=1, source_target_pairs={{0,16},{1,17},{2,18},{3,19},{4,20},{5,21},{6,22},{7,23},{8,24},{9,... | collective-permute-start | bytes 122888 | tf_op jit(solution)/shard_map/while/body/eval_jaxpr/ppermute | solution.py:16
  273.2 4.2 %collective-permute-start = (bf16[32,640]{1,0:T(8,128)(2,1)S(1)}, bf16[32,640]{1,0:T(8,128)(2,1)S(1)}, u32[]{:S(2)}, u32[]{:S(2)}) collective-permute-start(bf16[32,640]{1,0:T(8,128)(2,1)S(1)} %get-tuple-element.325), channel_id=1, source_target_pairs={{0,16},{1,17},{2,18},{3,19},{4,20},{5,21},{6,22},{7,23},{8,24},{9,... | collective-permute-start | bytes 122888 | tf_op jit(solution)/shard_map/while/body/eval_jaxpr/ppermute | solution.py:16
where the time goes:
time: 290 us; the launch traced here: 286 us
  local copies, waits for them, and re-layouts  84.2 us (29%)
  blocking collectives  65.2 us (22%)
  matrix products  55.5 us (19%)
  loops' own time  30.8 us (11%)
  waiting for transfers between devices  26.5 us (9%)
  starting transfers between devices  15.9 us (5%)
  other arithmetic  7.65 us (3%)
    all_gather x9, blocking collectives, tick_columns(): gathered = lax.all_gather(own_rows, 'seq', axis=1, tiled=True)  57 us
    dot_general x9, matrix products, project(): jnp.dot(normed, weights, preferred_element_type=jnp.float32)  50.4 us
    unnamed x11, local copies, waits for them, and re-layouts  34.1 us
    another operation x1, loops' own time, local(): lax.scan(tick_columns, start_carry, jnp.arange(tick_count, dtype=jnp.int32))  30.8 us
    ppermute x9, waiting for transfers between devices, shifted(): return lax.ppermute(value, axis, pairs)  26.5 us
    while x3, local copies, waits for them, and re-layouts, local(): lax.scan(tick_columns, start_carry, jnp.arange(tick_count, dtype=jnp.int32))  14.7 us
    ppermute x9, starting transfers between devices, shifted(): return lax.ppermute(value, axis, pairs)  11.6 us
    all_to_all x1, blocking collectives, local(): lax.all_to_all(final_carry[2], 'seq', split_axis=1, concat_axis=2, tiled=...  8.2 us
  transfers between devices with their start and end apart: 10, of which 9 were waited for; matrix products, arithmetic and copies ran while one was open for 11% of the time, Pallas kernels for 0%

commit v1 on v0

v1 whole, which is shorter than its diff:
```python
import functools

import jax
import jax.numpy as jnp
from jax import lax
from jax.experimental import pallas as pl
from jax.experimental.pallas import tpu as pltpu
from jax.sharding import PartitionSpec as P

HEAD_DIM = 128
TILES_P = 2
EPSILON = 1e-06
MASKED = 1e30
MESH = pl.DeviceIdType.MESH
ROW_CHUNK = 16


def dot_t(a, b, dims):
    return lax.dot_general(a, b, (dims, ((), ())), preferred_element_type=jnp.float32)


def kernel(
    sizes,
    timestep_ref,
    order_ref,
    latent_ref,
    weights_ref,
    modulation_ref,
    tiles_ref,
    stale_ref,
    out_ref,
    hidden,
    normed,
    weights,
    stale,
    mods,
    bias,
    result,
    weight_sem,
    stale_sem,
    own_sem,
    lat_send,
    lat_recv,
    next_send,
    next_recv,
    out_send,
    out_recv,
    back_send,
    back_recv,
):
    patches, rows_dev, seq_count, pipe_count, heads = sizes
    stage = lax.axis_index("pipe")
    me = lax.axis_index("seq")
    last = pipe_count - 1
    block = patches * rows_dev
    tokens = block * seq_count
    local_w = heads * HEAD_DIM
    tile_len = rows_dev * seq_count // TILES_P
    ntiles = patches * TILES_P

    def rows_of(rank):
        return pl.ds(pl.multiple_of(rank * block, block), block)

    def columns_of(rank, head):
        return pl.ds(pl.multiple_of(rank * local_w + head * HEAD_DIM, HEAD_DIM), HEAD_DIM)

    def peer(step):
        return lax.rem(me + step, seq_count)

    def weight_copy(head, part):
        return pltpu.make_async_copy(
            weights_ref.at[part, :, pl.ds(head * HEAD_DIM, HEAD_DIM)],
            weights.at[head, :, pl.ds(part * HEAD_DIM, HEAD_DIM)],
            weight_sem.at[head, part],
        )

    def stale_copy():
        return pltpu.make_async_copy(stale_ref, stale, stale_sem)

    def own_latent():
        return pltpu.make_async_copy(latent_ref, hidden.at[rows_of(me)], own_sem)

    def latent_copy(step):
        return pltpu.make_async_remote_copy(
            src_ref=latent_ref,
            dst_ref=hidden.at[rows_of(me)],
            send_sem=lat_send.at[step],
            recv_sem=lat_recv.at[me],
            device_id={"seq": peer(step)},
            device_id_type=MESH,
        )

    def latent_arrival(source):
        return pltpu.make_async_remote_copy(
            src_ref=latent_ref,
            dst_ref=hidden.at[rows_of(source)],
            send_sem=lat_send.at[0],
            recv_sem=lat_recv.at[source],
            device_id={"seq": source},
            device_id_type=MESH,
        )

    def next_copy(head, step):
        return pltpu.make_async_remote_copy(
            src_ref=result.at[head],
            dst_ref=hidden.at[:, columns_of(me, head)],
            send_sem=next_send.at[head, step],
            recv_sem=next_recv.at[head, me],
            device_id={"pipe": stage + 1, "seq": peer(step)},
            device_id_type=MESH,
        )

    def next_arrival(head, source):
        return pltpu.make_async_remote_copy(
            src_ref=result.at[head],
            dst_ref=hidden.at[:, columns_of(source, head)],
            send_sem=next_send.at[head, 0],
            recv_sem=next_recv.at[head, source],
            device_id={"pipe": stage - 1, "seq": source},
            device_id_type=MESH,
        )

    def back_copy(target):
        return pltpu.make_async_remote_copy(
            src_ref=hidden.at[rows_of(me)],
            dst_ref=out_ref,
            send_sem=back_send,
            recv_sem=back_recv,
            device_id={"pipe": target},
            device_id_type=MESH,
        )

    def out_copy(head, step):
        return pltpu.make_async_remote_copy(
            src_ref=result.at[head, rows_of(peer(step))],
            dst_ref=out_ref.at[:, columns_of(me, head)],
            send_sem=out_send.at[head, step],
            recv_sem=out_recv.at[head, me],
            device_id={"seq": peer(step)},
            device_id_type=MESH,
        )

    def out_arrival(head, source):
        return pltpu.make_async_remote_copy(
            src_ref=result.at[head, rows_of(source)],
            dst_ref=out_ref.at[:, columns_of(source, head)],
            send_sem=out_send.at[head, 0],
            recv_sem=out_recv.at[head, source],
            device_id={"seq": source},
            device_id_type=MESH,
        )

    def out_own(head):
        return pltpu.make_async_copy(
            result.at[head, rows_of(me)],
            out_ref.at[:, columns_of(me, head)],
            out_send.at[head, 0],
        )

    barrier = pltpu.get_barrier_semaphore()
    for step in range(1, seq_count):
        pl.semaphore_signal(barrier, inc=1, device_id={"seq": peer(step)}, device_id_type=MESH)

    @pl.when(stage > 0)
    def _():
        for step in range(seq_count):
            pl.semaphore_signal(
                barrier, inc=1, device_id={"pipe": stage - 1, "seq": peer(step)}, device_id_type=MESH
            )

    @pl.when(stage < last)
    def _():
        for step in range(seq_count):
            pl.semaphore_signal(
                barrier, inc=1, device_id={"pipe": stage + 1, "seq": peer(step)}, device_id_type=MESH
            )

    @pl.when(stage == 0)
    def _():
        own_latent().start()

    for head in range(heads):
        for part in range(3):
            weight_copy(head, part).start()
    stale_copy().start()

    neighbours = (
        seq_count - 1
        + jnp.where(stage > 0, seq_count, 0)
        + jnp.where(stage < last, seq_count, 0)
    )
    pl.semaphore_wait(barrier, neighbours)

    @pl.when(stage == 0)
    def _():
        for step in range(1, seq_count):
            latent_copy(step).start()

    picked_step = lax.broadcasted_iota(jnp.int32, modulation_ref.shape[1:], 0) == timestep_ref[0]
    for part in range(3):
        row = jnp.sum(jnp.where(picked_step, modulation_ref[part], 0.0), axis=0, keepdims=True)
        mods[pl.ds(part, 1), :] = row + 1.0 if part == 1 else row

    key_tile = lax.broadcasted_iota(jnp.int32, (ntiles, ntiles), 0)
    query_tile = lax.broadcasted_iota(jnp.int32, (ntiles, ntiles), 1)
    chosen = jnp.zeros((ntiles, ntiles), jnp.float32)
    for j in range(tiles_ref.shape[0]):
        chosen = chosen + jnp.where(tiles_ref[pl.ds(j, 1), :] == key_tile, 1.0, 0.0)
    key_place = jnp.zeros((ntiles, ntiles), jnp.int32)
    query_place = jnp.zeros((ntiles, ntiles), jnp.int32)
    for t in range(patches):
        key_place = jnp.where(lax.div(key_tile, TILES_P) == order_ref[t], t, key_place)
        query_place = jnp.where(lax.div(query_tile, TILES_P) == order_ref[t], t, query_place)
    fresh = jnp.where(key_place <= query_place, chosen, 0.0)

    row_id = lax.broadcasted_iota(jnp.int32, (tokens, ntiles), 0)
    tile_id = lax.broadcasted_iota(jnp.int32, (tokens, ntiles), 1)
    in_block = lax.rem(row_id, block)
    token = lax.div(row_id, block) * rows_dev + lax.rem(in_block, rows_dev)
    tile_of_row = lax.div(in_block, rows_dev) * TILES_P + lax.div(token, tile_len)
    by_seq = jnp.where(tile_of_row == tile_id, 1.0, 0.0).astype(jnp.bfloat16)
    by_patch = jnp.where(lax.div(row_id, tile_len) == tile_id, 1.0, 0.0).astype(jnp.bfloat16)
    for place, (table, keys) in enumerate(((fresh, by_seq), (chosen - fresh, by_patch))):
        per_query = dot_t(by_seq, table.astype(jnp.bfloat16), ((1,), (1,)))
        seen = dot_t(per_query.astype(jnp.bfloat16), keys, ((1,), (1,)))
        bias[place] = (seen - 1.0) * MASKED

    @pl.when(stage > 0)
    def _():
        def arrive(head, carry):
            for source in range(seq_count):
                next_arrival(head, source).wait_recv()
            return carry

        lax.fori_loop(0, heads, arrive, 0)
        back_copy(stage - 1).start()

    def normalize_block(step, carry):
        source = peer(step)

        @pl.when((stage == 0) & (step == 0))
        def _():
            own_latent().wait()

        @pl.when((stage == 0) & (step > 0))
        def _():
            latent_arrival(source).wait_recv()

        def normalize_rows(part, inner):
            rows = pl.ds(pl.multiple_of(source * block + part * ROW_CHUNK, ROW_CHUNK), ROW_CHUNK)
            floated = hidden[rows, :].astype(jnp.float32)
            centred = floated - jnp.mean(floated, axis=-1, keepdims=True)
            spread = jnp.mean(centred * centred, axis=-1, keepdims=True)
            normed[rows, :] = (
                centred * lax.rsqrt(spread + EPSILON) * mods[1:2, :] + mods[0:1, :]
            ).astype(jnp.bfloat16)
            return inner

        return lax.fori_loop(0, block // ROW_CHUNK, normalize_rows, carry)

    lax.fori_loop(0, seq_count, normalize_block, 0)
    stale_copy().wait()

    def one_head(head, carry):
        for part in range(3):
            weight_copy(head, part).wait()
        projected = jnp.dot(
            normed[...], weights[head], preferred_element_type=jnp.float32
        ).astype(jnp.bfloat16)
        query = projected[:, :HEAD_DIM]
        key = projected[:, HEAD_DIM : 2 * HEAD_DIM]
        value = projected[:, 2 * HEAD_DIM :]
        lanes = pl.ds(pl.multiple_of(head * HEAD_DIM, HEAD_DIM), HEAD_DIM)
        scale = HEAD_DIM ** (-0.5)
        fresh_s = dot_t(query, key, ((1,), (1,))) * scale + bias[0]
        stale_s = dot_t(query, stale[0, :, lanes], ((1,), (1,))) * scale + bias[1]
        largest = jnp.maximum(
            jnp.max(fresh_s, axis=-1, keepdims=True), jnp.max(stale_s, axis=-1, keepdims=True)
        )
        fresh_p = jnp.exp(fresh_s - largest)
        stale_p = jnp.exp(stale_s - largest)
        total = jnp.sum(fresh_p, axis=-1, keepdims=True) + jnp.sum(stale_p, axis=-1, keepdims=True)
        mixed = jnp.dot(
            fresh_p.astype(jnp.bfloat16), value, preferred_element_type=jnp.float32
        ) + jnp.dot(
            stale_p.astype(jnp.bfloat16), stale[1, :, lanes], preferred_element_type=jnp.float32
        )
        attended = (mixed / total).astype(jnp.bfloat16).astype(jnp.float32)
        mine = columns_of(me, head)
        result[head] = (
            hidden[:, mine].astype(jnp.float32) + mods[2:3, mine] * attended
        ).astype(jnp.bfloat16)

        @pl.when(stage < last)
        def _():
            for step in range(seq_count):
                next_copy(head, step).start()

        @pl.when(stage == last)
        def _():
            for step in range(1, seq_count):
                out_copy(head, step).start()
            out_own(head).start()

        return carry

    lax.fori_loop(0, heads, one_head, 0)

    @pl.when(stage == 0)
    def _():
        for step in range(1, seq_count):
            latent_copy(step).wait_send()

    @pl.when(stage > 0)
    def _():
        back_copy(stage - 1).wait_send()

    @pl.when(stage < last)
    def _():
        def sent(head, carry):
            for step in range(seq_count):
                next_copy(head, step).wait_send()
            return carry

        lax.fori_loop(0, heads, sent, 0)
        back_copy(stage + 1).wait_recv()

    @pl.when(stage == last)
    def _():
        def done(head, carry):
            out_own(head).wait()
            for step in range(1, seq_count):
                out_copy(head, step).wait_send()
                out_arrival(head, peer(step)).wait_recv()
            return carry

        lax.fori_loop(0, heads, done, 0)


def local(latent, w_qkv, modulation, timestep, order, tiles, stale_kv):
    patches, rows_dev, width = latent.shape
    local_w = w_qkv.shape[3]
    heads = local_w // HEAD_DIM
    seq_count = lax.axis_size("seq")
    pipe_count = lax.axis_size("pipe")
    block = patches * rows_dev
    tokens = block * seq_count
    weights = jnp.transpose(w_qkv[0], (1, 0, 2))
    stale = jnp.transpose(stale_kv[0].reshape(tokens, 2, local_w), (1, 0, 2))
    mods = jnp.transpose(modulation[0], (1, 0, 2))
    smem = pl.BlockSpec(memory_space=pltpu.SMEM)
    vmem = pl.BlockSpec(memory_space=pltpu.VMEM)
    anywhere = pl.BlockSpec(memory_space=pl.ANY)
    bf16 = jnp.bfloat16
    dma = pltpu.SemaphoreType.DMA
    finished = pl.pallas_call(
        functools.partial(kernel, (patches, rows_dev, seq_count, pipe_count, heads)),
        out_shape=jax.ShapeDtypeStruct((block, width), bf16),
        in_specs=[smem, smem, anywhere, anywhere, vmem, vmem, anywhere],
        out_specs=anywhere,
        scratch_shapes=[
            pltpu.VMEM((tokens, width), bf16),
            pltpu.VMEM((tokens, width), bf16),
            pltpu.VMEM((heads, width, 3 * HEAD_DIM), bf16),
            pltpu.VMEM((2, tokens, local_w), bf16),
            pltpu.VMEM((8, width), jnp.float32),
            pltpu.VMEM((2, tokens, tokens), jnp.float32),
            pltpu.VMEM((heads, tokens, HEAD_DIM), bf16),
            dma((heads, 3)),
            dma(()),
            dma(()),
            dma((seq_count,)),
            dma((seq_count,)),
            dma((heads, seq_count)),
            dma((heads, seq_count)),
            dma((heads, seq_count)),
            dma((heads, seq_count)),
            dma(()),
            dma(()),
        ],
        compiler_params=pltpu.CompilerParams(
            collective_id=0, has_side_effects=True, vmem_limit_bytes=56 * 1024 * 1024
        ),
    )(timestep, order, latent.reshape(block, width), weights, mods, tiles.T, stale)
    return finished.reshape(1, patches, rows_dev, width)


def solution(mesh):
    return jax.shard_map(
        local,
        mesh=mesh,
        in_specs=(
            P("batch", "seq", None),
            P("pipe", None, None, "seq"),
            P("pipe", None, None, None),
            P(),
            P("batch"),
            P("batch", None),
            P("pipe", "batch", None, None, "seq"),
        ),
        out_specs=P("pipe", "batch", "seq", None),
        check_vma=False,
    )
```

time: 290 us -> 46.3 us (0.16); the launches traced: 286 us -> 46.1 us
  local copies, waits for them, and re-layouts: 84.2 us -> 3.72 us
  blocking collectives: 65.2 us -> 0 us
  matrix products: 55.5 us -> 0 us
  Pallas kernels: 0 us -> 41.7 us
  loops' own time: 30.8 us -> 0 us
  waiting for transfers between devices: 26.5 us -> 0 us
  starting transfers between devices: 15.9 us -> 0 us
  other arithmetic: 7.65 us -> 0 us
    all_gather x9 -> x0, blocking collectives: 57 us -> none  [tick_columns(): gathered = lax.all_gather(own_rows, 'seq', axis=1, tiled=True)]
    dot_general x27 -> x0, matrix products: 55.5 us -> none  [the longest x9 50.4 us: project(): jnp.dot(normed, weights, preferred_element_type=jnp.float32)]
    pallas_call x0 -> x1, Pallas kernels: none -> 41.7 us  [local(): pl.pallas_call(functools.partial(kernel, (patches, rows_dev, seq_count, p...]
    another operation x1 -> x0, loops' own time: 30.8 us -> none  [local(): lax.scan(tick_columns, start_carry, jnp.arange(tick_count, dtype=jnp.int32))]
    unnamed x11 -> x2, local copies, waits for them, and re-layouts: 34.1 us -> 3.72 us
    ppermute x9 -> x0, waiting for transfers between devices: 26.5 us -> none  [shifted(): return lax.ppermute(value, axis, pairs)]
    while x3 -> x0, local copies, waits for them, and re-layouts: 14.7 us -> none  [local(): lax.scan(tick_columns, start_carry, jnp.arange(tick_count, dtype=jnp.int32))]
    ppermute x9 -> x0, starting transfers between devices: 11.6 us -> none  [shifted(): return lax.ppermute(value, axis, pairs)]
  transfers between devices with their start and end apart: 10 -> 0, of which waited for: 9 -> 0; matrix products, arithmetic and copies ran while one was open for 11% -> 0% of each run, Pallas kernels for 0% -> 0%
where the time goes in v1:
time: 46.3 us; the launch traced here: 46.1 us
  Pallas kernels  41.7 us (90%)
  local copies, waits for them, and re-layouts  3.72 us (8%)
  between operations  0.66 us (1%)
    pallas_call x1, Pallas kernels, local(): pl.pallas_call(functools.partial(kernel, (patches, rows_dev, seq_count, p...  41.7 us
    unnamed x2, local copies, waits for them, and re-layouts  3.72 us

profile of v1, /device:TPU:1, one launch (start us, length us, event | category | flops | bytes accessed | tf_op | source)
XLA Modules:
  0.0 46.1 jit_solution(13417760620092797364)
XLA Ops:
  0.7 2.0 %copy.8 = bf16[1,8,32,2,640]{4,2,1,3,0:T(8,128)(2,1)} copy(bf16[1,8,32,2,640]{4,3,2,1,0:T(2,128)(2,1)} %param.13) | data formatting | bytes 1310720 | tf_op args[6]
  2.6 41.7 %shard_map.73 = bf16[64,2560]{1,0:T(8,128)(2,1)} custom-call(s32[1]{0:T(128)S(6)} %copy.10.timestep_ref, s32[8]{0:T(128)} %order_ref.1, bf16[64,2560]{1,0:T(8,128)(2,1)} %bitcast.15, bf16[3,2560,640]{2,1,0:T(8,128)(2,1)} %bitcast.12, f32[3,8,2560]{2,1,0:T(8,128)} %bitcast.16, s32[6,16]{1,0:T(8,128)} %bitcast.17, bf16[2,256,640]{2,1,0:T(8,128)(2,1)} %bitcast.13), custom_call_target="tpu_custom_call" | custom-call | tf_op jit(solution)/shard_map/pallas_call | solution.py:356
  44.4 1.7 %copy.11 = bf16[1,8,8,2560]{3,2,1,0:T(8,128)(2,1)} copy(bf16[1,8,8,2560]{3,2,1,0:T(8,128)(2,1)} %bitcast.14) | data formatting | bytes 655360

commit v2 on v1

--- a/solution.py
+++ b/solution.py
@@ -11,6 +11,7 @@
 TILES_P = 2
 EPSILON = 1e-06
 MASKED = 1e30
+LOG2E = 1.4426950408889634
 MESH = pl.DeviceIdType.MESH
 ROW_CHUNK = 16
 
@@ -36,6 +37,7 @@
     mods,
     bias,
     result,
+    qkv,
     weight_sem,
     stale_sem,
     own_sem,
@@ -70,7 +72,7 @@
     def weight_copy(head, part):
         return pltpu.make_async_copy(
             weights_ref.at[part, :, pl.ds(head * HEAD_DIM, HEAD_DIM)],
-            weights.at[head, :, pl.ds(part * HEAD_DIM, HEAD_DIM)],
+            weights.at[:, pl.ds((head * 3 + part) * HEAD_DIM, HEAD_DIM)],
             weight_sem.at[head, part],
         )
 
@@ -246,7 +248,7 @@
         def _():
             latent_arrival(source).wait_recv()
 
-        def normalize_rows(part, inner):
+        def normalize_rows(part):
             rows = pl.ds(pl.multiple_of(source * block + part * ROW_CHUNK, ROW_CHUNK), ROW_CHUNK)
             floated = hidden[rows, :].astype(jnp.float32)
             centred = floated - jnp.mean(floated, axis=-1, keepdims=True)
@@ -254,34 +256,45 @@
             normed[rows, :] = (
                 centred * lax.rsqrt(spread + EPSILON) * mods[1:2, :] + mods[0:1, :]
             ).astype(jnp.bfloat16)
-            return inner
-
-        return lax.fori_loop(0, block // ROW_CHUNK, normalize_rows, carry)
+
+        for part in range(block // ROW_CHUNK):
+            normalize_rows(part)
+        return carry
 
     lax.fori_loop(0, seq_count, normalize_block, 0)
     stale_copy().wait()
 
-    def one_head(head, carry):
-        for part in range(3):
-            weight_copy(head, part).wait()
+    def project(group):
+        for head in group:
+            for part in range(3):
+                weight_copy(head, part).wait()
+        first, count = group[0], len(group)
         projected = jnp.dot(
-            normed[...], weights[head], preferred_element_type=jnp.float32
-        ).astype(jnp.bfloat16)
-        query = projected[:, :HEAD_DIM]
-        key = projected[:, HEAD_DIM : 2 * HEAD_DIM]
-        value = projected[:, 2 * HEAD_DIM :]
-        lanes = pl.ds(pl.multiple_of(head * HEAD_DIM, HEAD_DIM), HEAD_DIM)
-        scale = HEAD_DIM ** (-0.5)
-        fresh_s = dot_t(query, key, ((1,), (1,))) * scale + bias[0]
-        stale_s = dot_t(query, stale[0, :, lanes], ((1,), (1,))) * scale + bias[1]
+            normed[...],
+            weights[:, first * 3 * HEAD_DIM : (first + count) * 3 * HEAD_DIM],
+            preferred_element_type=jnp.float32,
+        )
+        for place, head in enumerate(group):
+            base = place * 3 * HEAD_DIM
+            query = projected[:, base : base + HEAD_DIM] * (HEAD_DIM ** (-0.5) * LOG2E)
+            qkv[head, 0] = query.astype(jnp.bfloat16)
+            for part in (1, 2):
+                piece = projected[:, base + part * HEAD_DIM : base + (part + 1) * HEAD_DIM]
+                qkv[head, part] = piece.astype(jnp.bfloat16)
+
+    def attend(head):
+        query = qkv[head, 0]
+        lanes = slice(head * HEAD_DIM, (head + 1) * HEAD_DIM)
+        fresh_s = dot_t(query, qkv[head, 1], ((1,), (1,))) + bias[0]
+        stale_s = dot_t(query, stale[0, :, lanes], ((1,), (1,))) + bias[1]
         largest = jnp.maximum(
             jnp.max(fresh_s, axis=-1, keepdims=True), jnp.max(stale_s, axis=-1, keepdims=True)
         )
-        fresh_p = jnp.exp(fresh_s - largest)
-        stale_p = jnp.exp(stale_s - largest)
+        fresh_p = jnp.exp2(fresh_s - largest)
+        stale_p = jnp.exp2(stale_s - largest)
         total = jnp.sum(fresh_p, axis=-1, keepdims=True) + jnp.sum(stale_p, axis=-1, keepdims=True)
         mixed = jnp.dot(
-            fresh_p.astype(jnp.bfloat16), value, preferred_element_type=jnp.float32
+            fresh_p.astype(jnp.bfloat16), qkv[head, 2], preferred_element_type=jnp.float32
         ) + jnp.dot(
             stale_p.astype(jnp.bfloat16), stale[1, :, lanes], preferred_element_type=jnp.float32
         )
@@ -291,20 +304,28 @@
             hidden[:, mine].astype(jnp.float32) + mods[2:3, mine] * attended
         ).astype(jnp.bfloat16)
 
+    groups = [(0,)] + [
+        tuple(range(head, min(head + 2, heads))) for head in range(1, heads, 2)
+    ]
+    project(groups[0])
+    for place, group in enumerate(groups):
+        if place + 1 < len(groups):
+            project(groups[place + 1])
+        for head in group:
+            attend(head)
+
         @pl.when(stage < last)
         def _():
-            for step in range(seq_count):
-                next_copy(head, step).start()
+            for head in group:
+                for step in range(seq_count):
+                    next_copy(head, step).start()
 
         @pl.when(stage == last)
         def _():
-            for step in range(1, seq_count):
-                out_copy(head, step).start()
-            out_own(head).start()
-
-        return carry
-
-    lax.fori_loop(0, heads, one_head, 0)
+            for head in group:
+                for step in range(1, seq_count):
+                    out_copy(head, step).start()
+                out_own(head).start()
 
     @pl.when(stage == 0)
     def _():
@@ -361,11 +382,12 @@
         scratch_shapes=[
             pltpu.VMEM((tokens, width), bf16),
             pltpu.VMEM((tokens, width), bf16),
-            pltpu.VMEM((heads, width, 3 * HEAD_DIM), bf16),
+            pltpu.VMEM((width, heads * 3 * HEAD_DIM), bf16),
             pltpu.VMEM((2, tokens, local_w), bf16),
             pltpu.VMEM((8, width), jnp.float32),
             pltpu.VMEM((2, tokens, tokens), jnp.float32),
             pltpu.VMEM((heads, tokens, HEAD_DIM), bf16),
+            pltpu.VMEM((heads, 3, tokens, HEAD_DIM), bf16),
             dma((heads, 3)),
             dma(()),
             dma(()),

time: 46.3 us -> 42.3 us (0.914)
  Pallas kernels: 41.7 us -> 37.7 us
    pallas_call x1, Pallas kernels: 41.7 us -> 37.7 us  [local(): pl.pallas_call(functools.partial(kernel, (patches, rows_dev, seq_count, p...]
where the time goes in v2:
time: 42.3 us; the launch traced here: 42 us
  Pallas kernels  37.7 us (89%)
  local copies, waits for them, and re-layouts  3.72 us (9%)
  between operations  0.66 us (2%)
    pallas_call x1, Pallas kernels, local(): pl.pallas_call(functools.partial(kernel, (patches, rows_dev, seq_count, p...  37.7 us
    unnamed x2, local copies, waits for them, and re-layouts  3.72 us

profile of v2, /device:TPU:1, one launch (start us, length us, event | category | flops | bytes accessed | tf_op | source)
XLA Modules:
  0.0 42.0 jit_solution(5117993707125636934)
XLA Ops:
  0.7 2.0 %copy.8 = bf16[1,8,32,2,640]{4,2,1,3,0:T(8,128)(2,1)} copy(bf16[1,8,32,2,640]{4,3,2,1,0:T(2,128)(2,1)} %param.13) | data formatting | bytes 1310720 | tf_op args[6]
  2.6 37.7 %shard_map.73 = bf16[64,2560]{1,0:T(8,128)(2,1)} custom-call(s32[1]{0:T(128)S(6)} %copy.10.timestep_ref, s32[8]{0:T(128)} %order_ref.1, bf16[64,2560]{1,0:T(8,128)(2,1)} %bitcast.15, bf16[3,2560,640]{2,1,0:T(8,128)(2,1)} %bitcast.12, f32[3,8,2560]{2,1,0:T(8,128)} %bitcast.16, s32[6,16]{1,0:T(8,128)} %bitcast.17, bf16[2,256,640]{2,1,0:T(8,128)(2,1)} %bitcast.13), custom_call_target="tpu_custom_call" | custom-call | tf_op jit(solution)/shard_map/pallas_call | solution.py:377
  40.3 1.7 %copy.11 = bf16[1,8,8,2560]{3,2,1,0:T(8,128)(2,1)} copy(bf16[1,8,8,2560]{3,2,1,0:T(8,128)(2,1)} %bitcast.14) | data formatting | bytes 655360

commit v3 on v2

--- a/solution.py
+++ b/solution.py
@@ -30,9 +30,12 @@
     tiles_ref,
     stale_ref,
     out_ref,
+    arrived,
     hidden,
     normed,
     weights,
+    raw_stale,
+    mixed_stale,
     stale,
     mods,
     bias,
@@ -59,12 +62,16 @@
     local_w = heads * HEAD_DIM
     tile_len = rows_dev * seq_count // TILES_P
     ntiles = patches * TILES_P
+    columns = seq_count * heads
 
     def rows_of(rank):
         return pl.ds(pl.multiple_of(rank * block, block), block)
 
     def columns_of(rank, head):
         return pl.ds(pl.multiple_of(rank * local_w + head * HEAD_DIM, HEAD_DIM), HEAD_DIM)
+
+    def place_of(rank, head):
+        return rank * heads + head
 
     def peer(step):
         return lax.rem(me + step, seq_count)
@@ -77,15 +84,15 @@
         )
 
     def stale_copy():
-        return pltpu.make_async_copy(stale_ref, stale, stale_sem)
+        return pltpu.make_async_copy(stale_ref, raw_stale, stale_sem)
 
     def own_latent():
-        return pltpu.make_async_copy(latent_ref, hidden.at[rows_of(me)], own_sem)
+        return pltpu.make_async_copy(latent_ref, arrived.at[rows_of(me)], own_sem)
 
     def latent_copy(step):
         return pltpu.make_async_remote_copy(
             src_ref=latent_ref,
-            dst_ref=hidden.at[rows_of(me)],
+            dst_ref=arrived.at[rows_of(me)],
             send_sem=lat_send.at[step],
             recv_sem=lat_recv.at[me],
             device_id={"seq": peer(step)},
@@ -95,7 +102,7 @@
     def latent_arrival(source):
         return pltpu.make_async_remote_copy(
             src_ref=latent_ref,
-            dst_ref=hidden.at[rows_of(source)],
+            dst_ref=arrived.at[rows_of(source)],
             send_sem=lat_send.at[0],
             recv_sem=lat_recv.at[source],
             device_id={"seq": source},
@@ -105,7 +112,7 @@
     def next_copy(head, step):
         return pltpu.make_async_remote_copy(
             src_ref=result.at[head],
-            dst_ref=hidden.at[:, columns_of(me, head)],
+            dst_ref=hidden.at[place_of(me, head)],
             send_sem=next_send.at[head, step],
             recv_sem=next_recv.at[head, me],
             device_id={"pipe": stage + 1, "seq": peer(step)},
@@ -115,7 +122,7 @@
     def next_arrival(head, source):
         return pltpu.make_async_remote_copy(
             src_ref=result.at[head],
-            dst_ref=hidden.at[:, columns_of(source, head)],
+            dst_ref=hidden.at[place_of(source, head)],
             send_sem=next_send.at[head, 0],
             recv_sem=next_recv.at[head, source],
             device_id={"pipe": stage - 1, "seq": source},
@@ -124,7 +131,7 @@
 
     def back_copy(target):
         return pltpu.make_async_remote_copy(
-            src_ref=hidden.at[rows_of(me)],
+            src_ref=hidden.at[:, rows_of(me)],
             dst_ref=out_ref,
             send_sem=back_send,
             recv_sem=back_recv,
@@ -135,7 +142,7 @@
     def out_copy(head, step):
         return pltpu.make_async_remote_copy(
             src_ref=result.at[head, rows_of(peer(step))],
-            dst_ref=out_ref.at[:, columns_of(me, head)],
+            dst_ref=out_ref.at[place_of(me, head)],
             send_sem=out_send.at[head, step],
             recv_sem=out_recv.at[head, me],
             device_id={"seq": peer(step)},
@@ -145,7 +152,7 @@
     def out_arrival(head, source):
         return pltpu.make_async_remote_copy(
             src_ref=result.at[head, rows_of(source)],
-            dst_ref=out_ref.at[:, columns_of(source, head)],
+            dst_ref=out_ref.at[place_of(source, head)],
             send_sem=out_send.at[head, 0],
             recv_sem=out_recv.at[head, source],
             device_id={"seq": source},
@@ -155,7 +162,7 @@
     def out_own(head):
         return pltpu.make_async_copy(
             result.at[head, rows_of(me)],
-            out_ref.at[:, columns_of(me, head)],
+            out_ref.at[place_of(me, head)],
             out_send.at[head, 0],
         )
 
@@ -227,6 +234,16 @@
         seen = dot_t(per_query.astype(jnp.bfloat16), keys, ((1,), (1,)))
         bias[place] = (seen - 1.0) * MASKED
 
+    stale_copy().wait()
+    mixed_stale[...] = raw_stale[...].reshape(2 * tokens, local_w)
+    wanted = 2 * lax.broadcasted_iota(jnp.int32, (tokens, 2 * tokens), 0)
+    present = lax.broadcasted_iota(jnp.int32, (tokens, 2 * tokens), 1)
+    for part in range(2):
+        select = jnp.where(wanted + part == present, 1.0, 0.0).astype(jnp.bfloat16)
+        stale[part] = jnp.dot(
+            select, mixed_stale[...], preferred_element_type=jnp.float32
+        ).astype(jnp.bfloat16)
+
     @pl.when(stage > 0)
     def _():
         def arrive(head, carry):
@@ -237,32 +254,49 @@
         lax.fori_loop(0, heads, arrive, 0)
         back_copy(stage - 1).start()
 
-    def normalize_block(step, carry):
-        source = peer(step)
-
-        @pl.when((stage == 0) & (step == 0))
-        def _():
-            own_latent().wait()
-
-        @pl.when((stage == 0) & (step > 0))
-        def _():
-            latent_arrival(source).wait_recv()
-
-        def normalize_rows(part):
-            rows = pl.ds(pl.multiple_of(source * block + part * ROW_CHUNK, ROW_CHUNK), ROW_CHUNK)
-            floated = hidden[rows, :].astype(jnp.float32)
-            centred = floated - jnp.mean(floated, axis=-1, keepdims=True)
-            spread = jnp.mean(centred * centred, axis=-1, keepdims=True)
-            normed[rows, :] = (
-                centred * lax.rsqrt(spread + EPSILON) * mods[1:2, :] + mods[0:1, :]
-            ).astype(jnp.bfloat16)
-
+    def normalize_rows(rows, block_rows):
+        floated = block_rows.astype(jnp.float32)
+        centred = floated - jnp.mean(floated, axis=-1, keepdims=True)
+        spread = jnp.mean(centred * centred, axis=-1, keepdims=True)
+        normed[rows, :] = (
+            centred * lax.rsqrt(spread + EPSILON) * mods[1:2, :] + mods[0:1, :]
+        ).astype(jnp.bfloat16)
+
+    def row_chunks(source):
         for part in range(block // ROW_CHUNK):
-            normalize_rows(part)
-        return carry
-
-    lax.fori_loop(0, seq_count, normalize_block, 0)
-    stale_copy().wait()
+            yield pl.ds(pl.multiple_of(source * block + part * ROW_CHUNK, ROW_CHUNK), ROW_CHUNK)
+
+    @pl.when(stage == 0)
+    def _():
+        own_latent().wait()
+
+        def normalize_block(step, carry):
+            source = peer(step)
+
+            @pl.when(step > 0)
+            def _():
+                latent_arrival(source).wait_recv()
+
+            for rows in row_chunks(source):
+                block_rows = arrived[rows, :]
+                normalize_rows(rows, block_rows)
+                for place in range(columns):
+                    hidden[place, rows, :] = block_rows[:, place * HEAD_DIM : (place + 1) * HEAD_DIM]
+            return carry
+
+        lax.fori_loop(0, seq_count, normalize_block, 0)
+
+    @pl.when(stage > 0)
+    def _():
+        def normalize_block(source, carry):
+            for rows in row_chunks(source):
+                normalize_rows(
+                    rows,
+                    jnp.concatenate([hidden[place, rows, :] for place in range(columns)], axis=1),
+                )
+            return carry
+
+        lax.fori_loop(0, seq_count, normalize_block, 0)
 
     def project(group):
         for head in group:
@@ -301,7 +335,7 @@
         attended = (mixed / total).astype(jnp.bfloat16).astype(jnp.float32)
         mine = columns_of(me, head)
         result[head] = (
-            hidden[:, mine].astype(jnp.float32) + mods[2:3, mine] * attended
+            hidden[place_of(me, head)].astype(jnp.float32) + mods[2:3, mine] * attended
         ).astype(jnp.bfloat16)
 
     groups = [(0,)] + [
@@ -367,7 +401,7 @@
     block = patches * rows_dev
     tokens = block * seq_count
     weights = jnp.transpose(w_qkv[0], (1, 0, 2))
-    stale = jnp.transpose(stale_kv[0].reshape(tokens, 2, local_w), (1, 0, 2))
+    stale = stale_kv[0].reshape(tokens, 2, local_w)
     mods = jnp.transpose(modulation[0], (1, 0, 2))
     smem = pl.BlockSpec(memory_space=pltpu.SMEM)
     vmem = pl.BlockSpec(memory_space=pltpu.VMEM)
@@ -376,13 +410,16 @@
     dma = pltpu.SemaphoreType.DMA
     finished = pl.pallas_call(
         functools.partial(kernel, (patches, rows_dev, seq_count, pipe_count, heads)),
-        out_shape=jax.ShapeDtypeStruct((block, width), bf16),
+        out_shape=jax.ShapeDtypeStruct((seq_count * heads, block, HEAD_DIM), bf16),
         in_specs=[smem, smem, anywhere, anywhere, vmem, vmem, anywhere],
         out_specs=anywhere,
         scratch_shapes=[
             pltpu.VMEM((tokens, width), bf16),
+            pltpu.VMEM((seq_count * heads, tokens, HEAD_DIM), bf16),
             pltpu.VMEM((tokens, width), bf16),
             pltpu.VMEM((width, heads * 3 * HEAD_DIM), bf16),
+            pltpu.VMEM((tokens, 2, local_w), bf16),
+            pltpu.VMEM((2 * tokens, local_w), bf16),
             pltpu.VMEM((2, tokens, local_w), bf16),
             pltpu.VMEM((8, width), jnp.float32),
             pltpu.VMEM((2, tokens, tokens), jnp.float32),
@@ -404,7 +441,7 @@
             collective_id=0, has_side_effects=True, vmem_limit_bytes=56 * 1024 * 1024
         ),
     )(timestep, order, latent.reshape(block, width), weights, mods, tiles.T, stale)
-    return finished.reshape(1, patches, rows_dev, width)
+    return jnp.transpose(finished, (1, 0, 2)).reshape(1, patches, rows_dev, width)
 
 
 def solution(mesh):

time: 42.3 us -> 40.8 us (0.965)
  local copies, waits for them, and re-layouts: 3.72 us -> 2.12 us
    unnamed x2 -> x0, local copies, waits for them, and re-layouts: 3.72 us -> none
    transpose x0 -> x1, local copies, waits for them, and re-layouts: none -> 1.2 us  [local(): jnp.transpose(finished, (1, 0, 2)).reshape(1, patches, rows_dev, width)]
    reshape x0 -> x1, local copies, waits for them, and re-layouts: none -> 0.92 us  [local(): jnp.transpose(finished, (1, 0, 2)).reshape(1, patches, rows_dev, width)]
where the time goes in v3:
time: 40.8 us; the launch traced here: 40.7 us
  Pallas kernels  37.9 us (93%)
  local copies, waits for them, and re-layouts  2.12 us (5%)
  between operations  0.66 us (2%)
    pallas_call x1, Pallas kernels, local(): pl.pallas_call(functools.partial(kernel, (patches, rows_dev, seq_count, p...  37.9 us
    transpose x1, local copies, waits for them, and re-layouts, local(): jnp.transpose(finished, (1, 0, 2)).reshape(1, patches, rows_dev, width)  1.2 us
    reshape x1, local copies, waits for them, and re-layouts, local(): jnp.transpose(finished, (1, 0, 2)).reshape(1, patches, rows_dev, width)  0.92 us

profile of v3, /device:TPU:1, one launch (start us, length us, event | category | flops | bytes accessed | tf_op | source)
XLA Modules:
  0.0 40.7 jit_solution(5611245389961052873)
XLA Ops:
  0.7 37.9 %shard_map.73 = bf16[20,64,128]{2,1,0:T(8,128)(2,1)} custom-call(s32[1]{0:T(128)S(6)} %copy.9.timestep_ref, s32[8]{0:T(128)} %order_ref.1, bf16[64,2560]{1,0:T(8,128)(2,1)} %bitcast.13, bf16[3,2560,640]{2,1,0:T(8,128)(2,1)} %bitcast.10, f32[3,8,2560]{2,1,0:T(8,128)} %bitcast.14, s32[6,16]{1,0:T(8,128)} %bitcast.15, bf16[256,2,640]{2,1,0:T(2,128)(2,1)} %bitcast.12), custom_call_target="tpu_custom_call" | custom-call | tf_op jit(solution)/shard_map/pallas_call | solution.py:411
  38.5 1.2 %copy.8 = bf16[64,20,128]{2,1,0:T(8,128)(2,1)S(1)} copy(bf16[64,20,128]{2,0,1:T(8,128)(2,1)} %bitcast.11) | data formatting | bytes 655360 | tf_op jit(solution)/shard_map/transpose | solution.py:444
  39.7 0.9 %reshape.7 = bf16[1,8,8,2560]{3,2,1,0:T(8,128)(2,1)} reshape(bf16[64,20,128]{2,1,0:T(8,128)(2,1)S(1)} %copy.8) | data formatting | bytes 655360 | tf_op jit(solution)/shard_map/reshape | solution.py:444

commit v4 on v3

--- a/solution.py
+++ b/solution.py
@@ -76,12 +76,8 @@
     def peer(step):
         return lax.rem(me + step, seq_count)
 
-    def weight_copy(head, part):
-        return pltpu.make_async_copy(
-            weights_ref.at[part, :, pl.ds(head * HEAD_DIM, HEAD_DIM)],
-            weights.at[:, pl.ds((head * 3 + part) * HEAD_DIM, HEAD_DIM)],
-            weight_sem.at[head, part],
-        )
+    def weight_copy(part):
+        return pltpu.make_async_copy(weights_ref.at[part], weights.at[part], weight_sem.at[part])
 
     def stale_copy():
         return pltpu.make_async_copy(stale_ref, raw_stale, stale_sem)
@@ -187,11 +183,6 @@
     @pl.when(stage == 0)
     def _():
         own_latent().start()
-
-    for head in range(heads):
-        for part in range(3):
-            weight_copy(head, part).start()
-    stale_copy().start()
 
     neighbours = (
         seq_count - 1
@@ -204,6 +195,10 @@
     def _():
         for step in range(1, seq_count):
             latent_copy(step).start()
+
+    for part in range(3):
+        weight_copy(part).start()
+    stale_copy().start()
 
     picked_step = lax.broadcasted_iota(jnp.int32, modulation_ref.shape[1:], 0) == timestep_ref[0]
     for part in range(3):
@@ -298,23 +293,30 @@
 
         lax.fori_loop(0, seq_count, normalize_block, 0)
 
+    for part in range(3):
+        weight_copy(part).wait()
+
     def project(group):
-        for head in group:
-            for part in range(3):
-                weight_copy(head, part).wait()
-        first, count = group[0], len(group)
-        projected = jnp.dot(
-            normed[...],
-            weights[:, first * 3 * HEAD_DIM : (first + count) * 3 * HEAD_DIM],
-            preferred_element_type=jnp.float32,
-        )
-        for place, head in enumerate(group):
-            base = place * 3 * HEAD_DIM
-            query = projected[:, base : base + HEAD_DIM] * (HEAD_DIM ** (-0.5) * LOG2E)
-            qkv[head, 0] = query.astype(jnp.bfloat16)
-            for part in (1, 2):
-                piece = projected[:, base + part * HEAD_DIM : base + (part + 1) * HEAD_DIM]
-                qkv[head, part] = piece.astype(jnp.bfloat16)
+        lanes = slice(group[0] * HEAD_DIM, (group[-1] + 1) * HEAD_DIM)
+        span = len(group) * HEAD_DIM
+        pieces = [weights[part, :, lanes] for part in range(3)]
+        if len(group) == 1:
+            pieces = [jnp.concatenate(pieces, axis=1)]
+        projected = [
+            jnp.dot(normed[...], piece, preferred_element_type=jnp.float32) for piece in pieces
+        ]
+        for part in range(3):
+            whole = (
+                projected[part]
+                if len(projected) == 3
+                else projected[0][:, part * span : (part + 1) * span]
+            )
+            if part == 0:
+                whole = whole * (HEAD_DIM ** (-0.5) * LOG2E)
+            for place, head in enumerate(group):
+                qkv[head, part] = whole[:, place * HEAD_DIM : (place + 1) * HEAD_DIM].astype(
+                    jnp.bfloat16
+                )
 
     def attend(head):
         query = qkv[head, 0]
@@ -417,7 +419,7 @@
             pltpu.VMEM((tokens, width), bf16),
             pltpu.VMEM((seq_count * heads, tokens, HEAD_DIM), bf16),
             pltpu.VMEM((tokens, width), bf16),
-            pltpu.VMEM((width, heads * 3 * HEAD_DIM), bf16),
+            pltpu.VMEM((3, width, local_w), bf16),
             pltpu.VMEM((tokens, 2, local_w), bf16),
             pltpu.VMEM((2 * tokens, local_w), bf16),
             pltpu.VMEM((2, tokens, local_w), bf16),
@@ -425,7 +427,7 @@
             pltpu.VMEM((2, tokens, tokens), jnp.float32),
             pltpu.VMEM((heads, tokens, HEAD_DIM), bf16),
             pltpu.VMEM((heads, 3, tokens, HEAD_DIM), bf16),
-            dma((heads, 3)),
+            dma((3,)),
             dma(()),
             dma(()),
             dma((seq_count,)),

time: 40.8 us -> 40.4 us (level)
  Pallas kernels: 37.9 us -> 37.4 us
    pallas_call x1, Pallas kernels: 37.9 us -> 37.4 us  [local(): pl.pallas_call(functools.partial(kernel, (patches, rows_dev, seq_count, p...]
where the time goes in v4:
time: 40.4 us; the launch traced here: 40.2 us
  Pallas kernels  37.4 us (93%)
  local copies, waits for them, and re-layouts  2.12 us (5%)
  between operations  0.66 us (2%)
    pallas_call x1, Pallas kernels, local(): pl.pallas_call(functools.partial(kernel, (patches, rows_dev, seq_count, p...  37.4 us
    transpose x1, local copies, waits for them, and re-layouts, local(): jnp.transpose(finished, (1, 0, 2)).reshape(1, patches, rows_dev, width)  1.2 us
    reshape x1, local copies, waits for them, and re-layouts, local(): jnp.transpose(finished, (1, 0, 2)).reshape(1, patches, rows_dev, width)  0.92 us

profile of v4, /device:TPU:1, one launch (start us, length us, event | category | flops | bytes accessed | tf_op | source)
XLA Modules:
  0.0 40.2 jit_solution(12531536550376033683)
XLA Ops:
  0.7 37.4 %shard_map.73 = bf16[20,64,128]{2,1,0:T(8,128)(2,1)} custom-call(s32[1]{0:T(128)S(6)} %copy.9.timestep_ref, s32[8]{0:T(128)} %order_ref.1, bf16[64,2560]{1,0:T(8,128)(2,1)} %bitcast.13, bf16[3,2560,640]{2,1,0:T(8,128)(2,1)} %bitcast.10, f32[3,8,2560]{2,1,0:T(8,128)} %bitcast.14, s32[6,16]{1,0:T(8,128)} %bitcast.15, bf16[256,2,640]{2,1,0:T(2,128)(2,1)} %bitcast.12), custom_call_target="tpu_custom_call" | custom-call | tf_op jit(solution)/shard_map/pallas_call | solution.py:413
  38.1 1.2 %copy.8 = bf16[64,20,128]{2,1,0:T(8,128)(2,1)S(1)} copy(bf16[64,20,128]{2,0,1:T(8,128)(2,1)} %bitcast.11) | data formatting | bytes 655360 | tf_op jit(solution)/shard_map/transpose | solution.py:446
  39.3 0.9 %reshape.7 = bf16[1,8,8,2560]{3,2,1,0:T(8,128)(2,1)} reshape(bf16[64,20,128]{2,1,0:T(8,128)(2,1)S(1)} %copy.8) | data formatting | bytes 655360 | tf_op jit(solution)/shard_map/reshape | solution.py:446

commit v5 on v4

--- a/solution.py
+++ b/solution.py
@@ -48,6 +48,7 @@
     lat_recv,
     next_send,
     next_recv,
+    pass_send,
     out_send,
     out_recv,
     back_send,
@@ -73,6 +74,11 @@
     def place_of(rank, head):
         return rank * heads + head
 
+    square = 2
+    across_x = lax.div(me, square) * square + (square - 1 - lax.rem(me, square))
+    across_y = (square - 1 - lax.div(me, square)) * square + lax.rem(me, square)
+    diagonal = seq_count - 1 - me
+
     def peer(step):
         return lax.rem(me + step, seq_count)
 
@@ -85,44 +91,77 @@
     def own_latent():
         return pltpu.make_async_copy(latent_ref, arrived.at[rows_of(me)], own_sem)
 
-    def latent_copy(step):
-        return pltpu.make_async_remote_copy(
-            src_ref=latent_ref,
-            dst_ref=arrived.at[rows_of(me)],
-            send_sem=lat_send.at[step],
-            recv_sem=lat_recv.at[me],
-            device_id={"seq": peer(step)},
-            device_id_type=MESH,
-        )
-
-    def latent_arrival(source):
-        return pltpu.make_async_remote_copy(
-            src_ref=latent_ref,
-            dst_ref=arrived.at[rows_of(source)],
-            send_sem=lat_send.at[0],
-            recv_sem=lat_recv.at[source],
-            device_id={"seq": source},
-            device_id_type=MESH,
-        )
-
-    def next_copy(head, step):
-        return pltpu.make_async_remote_copy(
-            src_ref=result.at[head],
-            dst_ref=hidden.at[place_of(me, head)],
-            send_sem=next_send.at[head, step],
-            recv_sem=next_recv.at[head, me],
-            device_id={"pipe": stage + 1, "seq": peer(step)},
-            device_id_type=MESH,
-        )
-
-    def next_arrival(head, source):
-        return pltpu.make_async_remote_copy(
-            src_ref=result.at[head],
-            dst_ref=hidden.at[place_of(source, head)],
-            send_sem=next_send.at[head, 0],
-            recv_sem=next_recv.at[head, source],
-            device_id={"pipe": stage - 1, "seq": source},
-            device_id_type=MESH,
+    def half_of(rank, half, size):
+        return pl.ds(pl.multiple_of(rank * size + half * (size // 2), size // 2), size // 2)
+
+    def latent_copy(slot, half, target):
+        return pltpu.make_async_remote_copy(
+            src_ref=latent_ref.at[half_of(0, half, block)],
+            dst_ref=arrived.at[half_of(me, half, block)],
+            send_sem=lat_send.at[slot],
+            recv_sem=lat_recv.at[me, half],
+            device_id={"seq": target},
+            device_id_type=MESH,
+        )
+
+    def latent_pass(slot, source, half, target):
+        rows = half_of(source, half, block)
+        return pltpu.make_async_remote_copy(
+            src_ref=arrived.at[rows],
+            dst_ref=arrived.at[rows],
+            send_sem=lat_send.at[slot],
+            recv_sem=lat_recv.at[source, half],
+            device_id={"seq": target},
+            device_id_type=MESH,
+        )
+
+    def latent_sends():
+        return (
+            latent_copy(0, 0, across_x),
+            latent_copy(1, 1, across_y),
+            latent_copy(2, 1, across_x),
+            latent_copy(3, 0, across_y),
+        )
+
+    def latent_passes():
+        return latent_pass(4, across_x, 0, across_y), latent_pass(5, across_y, 1, across_x)
+
+    def next_copy(head, slot, half, target):
+        rows = half_of(0, half, tokens)
+        return pltpu.make_async_remote_copy(
+            src_ref=result.at[head, rows],
+            dst_ref=hidden.at[place_of(me, head), rows],
+            send_sem=next_send.at[head, slot],
+            recv_sem=next_recv.at[head, me, half],
+            device_id={"pipe": stage + 1, "seq": target},
+            device_id_type=MESH,
+        )
+
+    def next_sends(head):
+        return (
+            next_copy(head, 0, 0, across_x),
+            next_copy(head, 1, 1, across_y),
+            next_copy(head, 2, 1, across_x),
+            next_copy(head, 3, 0, across_y),
+            next_copy(head, 4, 0, me),
+            next_copy(head, 5, 1, me),
+        )
+
+    def next_pass(head, slot, source, half, target):
+        place = hidden.at[place_of(source, head), half_of(0, half, tokens)]
+        return pltpu.make_async_remote_copy(
+            src_ref=place,
+            dst_ref=place,
+            send_sem=pass_send.at[head, slot],
+            recv_sem=next_recv.at[head, source, half],
+            device_id={"seq": target},
+            device_id_type=MESH,
+        )
+
+    def next_passes(head):
+        return (
+            next_pass(head, 0, across_x, 0, across_y),
+            next_pass(head, 1, across_y, 1, across_x),
         )
 
     def back_copy(target):
@@ -193,17 +232,44 @@
 
     @pl.when(stage == 0)
     def _():
-        for step in range(1, seq_count):
-            latent_copy(step).start()
-
+        for copy in latent_sends():
+            copy.start()
+
+    stale_copy().start()
     for part in range(3):
         weight_copy(part).start()
-    stale_copy().start()
 
     picked_step = lax.broadcasted_iota(jnp.int32, modulation_ref.shape[1:], 0) == timestep_ref[0]
     for part in range(3):
         row = jnp.sum(jnp.where(picked_step, modulation_ref[part], 0.0), axis=0, keepdims=True)
         mods[pl.ds(part, 1), :] = row + 1.0 if part == 1 else row
+
+    def normalize_rows(rows, block_rows):
+        floated = block_rows.astype(jnp.float32)
+        centred = floated - jnp.mean(floated, axis=-1, keepdims=True)
+        spread = jnp.mean(centred * centred, axis=-1, keepdims=True)
+        normed[rows, :] = (
+            centred * lax.rsqrt(spread + EPSILON) * mods[1:2, :] + mods[0:1, :]
+        ).astype(jnp.bfloat16)
+
+    def row_chunks(source):
+        for part in range(block // ROW_CHUNK):
+            yield pl.ds(pl.multiple_of(source * block + part * ROW_CHUNK, ROW_CHUNK), ROW_CHUNK)
+
+    def normalize_latent(source):
+        for rows in row_chunks(source):
+            block_rows = arrived[rows, :]
+            normalize_rows(rows, block_rows)
+            for place in range(columns):
+                hidden[place, rows, :] = block_rows[:, place * HEAD_DIM : (place + 1) * HEAD_DIM]
+
+    @pl.when(stage == 0)
+    def _():
+        own_latent().wait()
+        normalize_latent(me)
+        for source, half, copy in zip((across_x, across_y), (0, 1), latent_passes()):
+            latent_pass(0, source, half, me).wait_recv()
+            copy.start()
 
     key_tile = lax.broadcasted_iota(jnp.int32, (ntiles, ntiles), 0)
     query_tile = lax.broadcasted_iota(jnp.int32, (ntiles, ntiles), 1)
@@ -241,45 +307,37 @@
 
     @pl.when(stage > 0)
     def _():
+        def pass_on(head, carry):
+            for source, half, copy in zip((across_x, across_y), (0, 1), next_passes(head)):
+                next_pass(head, 0, source, half, across_x).wait_recv()
+                copy.start()
+            return carry
+
         def arrive(head, carry):
-            for source in range(seq_count):
-                next_arrival(head, source).wait_recv()
+            for source, half in (
+                (me, 0),
+                (me, 1),
+                (across_x, 1),
+                (across_y, 0),
+                (diagonal, 0),
+                (diagonal, 1),
+            ):
+                next_pass(head, 0, source, half, across_x).wait_recv()
             return carry
 
+        lax.fori_loop(0, heads, pass_on, 0)
         lax.fori_loop(0, heads, arrive, 0)
         back_copy(stage - 1).start()
 
-    def normalize_rows(rows, block_rows):
-        floated = block_rows.astype(jnp.float32)
-        centred = floated - jnp.mean(floated, axis=-1, keepdims=True)
-        spread = jnp.mean(centred * centred, axis=-1, keepdims=True)
-        normed[rows, :] = (
-            centred * lax.rsqrt(spread + EPSILON) * mods[1:2, :] + mods[0:1, :]
-        ).astype(jnp.bfloat16)
-
-    def row_chunks(source):
-        for part in range(block // ROW_CHUNK):
-            yield pl.ds(pl.multiple_of(source * block + part * ROW_CHUNK, ROW_CHUNK), ROW_CHUNK)
-
     @pl.when(stage == 0)
     def _():
-        own_latent().wait()
-
-        def normalize_block(step, carry):
-            source = peer(step)
-
-            @pl.when(step > 0)
-            def _():
-                latent_arrival(source).wait_recv()
-
-            for rows in row_chunks(source):
-                block_rows = arrived[rows, :]
-                normalize_rows(rows, block_rows)
-                for place in range(columns):
-                    hidden[place, rows, :] = block_rows[:, place * HEAD_DIM : (place + 1) * HEAD_DIM]
-            return carry
-
-        lax.fori_loop(0, seq_count, normalize_block, 0)
+        latent_pass(0, across_x, 1, across_y).wait_recv()
+        normalize_latent(across_x)
+        latent_pass(0, across_y, 0, across_x).wait_recv()
+        normalize_latent(across_y)
+        latent_pass(0, diagonal, 0, across_x).wait_recv()
+        latent_pass(0, diagonal, 1, across_x).wait_recv()
+        normalize_latent(diagonal)
 
     @pl.when(stage > 0)
     def _():
@@ -353,8 +411,8 @@
         @pl.when(stage < last)
         def _():
             for head in group:
-                for step in range(seq_count):
-                    next_copy(head, step).start()
+                for copy in next_sends(head):
+                    copy.start()
 
         @pl.when(stage == last)
         def _():
@@ -365,18 +423,25 @@
 
     @pl.when(stage == 0)
     def _():
-        for step in range(1, seq_count):
-            latent_copy(step).wait_send()
+        for copy in latent_sends() + latent_passes():
+            copy.wait_send()
 
     @pl.when(stage > 0)
     def _():
         back_copy(stage - 1).wait_send()
 
+        def passed(head, carry):
+            for copy in next_passes(head):
+                copy.wait_send()
+            return carry
+
+        lax.fori_loop(0, heads, passed, 0)
+
     @pl.when(stage < last)
     def _():
         def sent(head, carry):
-            for step in range(seq_count):
-                next_copy(head, step).wait_send()
+            for copy in next_sends(head):
+                copy.wait_send()
             return carry
 
         lax.fori_loop(0, heads, sent, 0)
@@ -430,10 +495,11 @@
             dma((3,)),
             dma(()),
             dma(()),
-            dma((seq_count,)),
-            dma((seq_count,)),
-            dma((heads, seq_count)),
-            dma((heads, seq_count)),
+            dma((6,)),
+            dma((seq_count, 2)),
+            dma((heads, 6)),
+            dma((heads, seq_count, 2)),
+            dma((heads, 2)),
             dma((heads, seq_count)),
             dma((heads, seq_count)),
             dma(()),

time: 40.4 us -> 38.3 us (0.948)
  Pallas kernels: 37.4 us -> 35.4 us
    pallas_call x1, Pallas kernels: 37.4 us -> 35.4 us  [local(): pl.pallas_call(functools.partial(kernel, (patches, rows_dev, seq_count, p...]
where the time goes in v5:
time: 38.3 us; the launch traced here: 38.1 us
  Pallas kernels  35.4 us (92%)
  local copies, waits for them, and re-layouts  2.12 us (6%)
  between operations  0.66 us (2%)
    pallas_call x1, Pallas kernels, local(): pl.pallas_call(functools.partial(kernel, (patches, rows_dev, seq_count, p...  35.4 us
    transpose x1, local copies, waits for them, and re-layouts, local(): jnp.transpose(finished, (1, 0, 2)).reshape(1, patches, rows_dev, width)  1.2 us
    reshape x1, local copies, waits for them, and re-layouts, local(): jnp.transpose(finished, (1, 0, 2)).reshape(1, patches, rows_dev, width)  0.92 us

profile of v5, /device:TPU:1, one launch (start us, length us, event | category | flops | bytes accessed | tf_op | source)
XLA Modules:
  0.0 38.1 jit_solution(10097867771482327569)
XLA Ops:
  0.7 35.4 %shard_map.73 = bf16[20,64,128]{2,1,0:T(8,128)(2,1)} custom-call(s32[1]{0:T(128)S(6)} %copy.9.timestep_ref, s32[8]{0:T(128)} %order_ref.1, bf16[64,2560]{1,0:T(8,128)(2,1)} %bitcast.13, bf16[3,2560,640]{2,1,0:T(8,128)(2,1)} %bitcast.10, f32[3,8,2560]{2,1,0:T(8,128)} %bitcast.14, s32[6,16]{1,0:T(8,128)} %bitcast.15, bf16[256,2,640]{2,1,0:T(2,128)(2,1)} %bitcast.12), custom_call_target="tpu_custom_call" | custom-call | tf_op jit(solution)/shard_map/pallas_call | solution.py:478
  36.0 1.2 %copy.8 = bf16[64,20,128]{2,1,0:T(8,128)(2,1)S(1)} copy(bf16[64,20,128]{2,0,1:T(8,128)(2,1)} %bitcast.11) | data formatting | bytes 655360 | tf_op jit(solution)/shard_map/transpose | solution.py:512
  37.2 0.9 %reshape.7 = bf16[1,8,8,2560]{3,2,1,0:T(8,128)(2,1)} reshape(bf16[64,20,128]{2,1,0:T(8,128)(2,1)S(1)} %copy.8) | data formatting | bytes 655360 | tf_op jit(solution)/shard_map/reshape | solution.py:512

commit v6 on v5

--- a/solution.py
+++ b/solution.py
@@ -164,20 +164,27 @@
             next_pass(head, 1, across_y, 1, across_x),
         )
 
-    def back_copy(target):
-        return pltpu.make_async_remote_copy(
-            src_ref=hidden.at[:, rows_of(me)],
-            dst_ref=out_ref,
-            send_sem=back_send,
-            recv_sem=back_recv,
+    def back_copy(place, target):
+        return pltpu.make_async_remote_copy(
+            src_ref=hidden.at[place, rows_of(me)],
+            dst_ref=out_ref.at[:, columns_of(0, place)],
+            send_sem=back_send.at[place],
+            recv_sem=back_recv.at[place],
             device_id={"pipe": target},
             device_id_type=MESH,
         )
 
+    def each_back(act):
+        def one(place, carry):
+            act(place)
+            return carry
+
+        lax.fori_loop(0, columns, one, 0)
+
     def out_copy(head, step):
         return pltpu.make_async_remote_copy(
             src_ref=result.at[head, rows_of(peer(step))],
-            dst_ref=out_ref.at[place_of(me, head)],
+            dst_ref=out_ref.at[:, columns_of(me, head)],
             send_sem=out_send.at[head, step],
             recv_sem=out_recv.at[head, me],
             device_id={"seq": peer(step)},
@@ -187,7 +194,7 @@
     def out_arrival(head, source):
         return pltpu.make_async_remote_copy(
             src_ref=result.at[head, rows_of(source)],
-            dst_ref=out_ref.at[place_of(source, head)],
+            dst_ref=out_ref.at[:, columns_of(source, head)],
             send_sem=out_send.at[head, 0],
             recv_sem=out_recv.at[head, source],
             device_id={"seq": source},
@@ -197,7 +204,7 @@
     def out_own(head):
         return pltpu.make_async_copy(
             result.at[head, rows_of(me)],
-            out_ref.at[place_of(me, head)],
+            out_ref.at[:, columns_of(me, head)],
             out_send.at[head, 0],
         )
 
@@ -327,7 +334,7 @@
 
         lax.fori_loop(0, heads, pass_on, 0)
         lax.fori_loop(0, heads, arrive, 0)
-        back_copy(stage - 1).start()
+        each_back(lambda place: back_copy(place, stage - 1).start())
 
     @pl.when(stage == 0)
     def _():
@@ -386,40 +393,48 @@
         )
         fresh_p = jnp.exp2(fresh_s - largest)
         stale_p = jnp.exp2(stale_s - largest)
-        total = jnp.sum(fresh_p, axis=-1, keepdims=True) + jnp.sum(stale_p, axis=-1, keepdims=True)
+        ones = jnp.ones((tokens, HEAD_DIM), jnp.bfloat16)
         mixed = jnp.dot(
-            fresh_p.astype(jnp.bfloat16), qkv[head, 2], preferred_element_type=jnp.float32
+            fresh_p.astype(jnp.bfloat16),
+            jnp.concatenate([qkv[head, 2], ones], axis=1),
+            preferred_element_type=jnp.float32,
         ) + jnp.dot(
-            stale_p.astype(jnp.bfloat16), stale[1, :, lanes], preferred_element_type=jnp.float32
-        )
-        attended = (mixed / total).astype(jnp.bfloat16).astype(jnp.float32)
+            stale_p.astype(jnp.bfloat16),
+            jnp.concatenate([stale[1, :, lanes], ones], axis=1),
+            preferred_element_type=jnp.float32,
+        )
+        attended = (mixed[:, :HEAD_DIM] / mixed[:, HEAD_DIM:]).astype(jnp.bfloat16).astype(jnp.float32)
         mine = columns_of(me, head)
         result[head] = (
             hidden[place_of(me, head)].astype(jnp.float32) + mods[2:3, mine] * attended
         ).astype(jnp.bfloat16)
 
+    def send(head):
+        @pl.when(stage < last)
+        def _():
+            for copy in next_sends(head):
+                copy.start()
+
+        @pl.when(stage == last)
+        def _():
+            for step in range(1, seq_count):
+                out_copy(head, step).start()
+            out_own(head).start()
+
     groups = [(0,)] + [
         tuple(range(head, min(head + 2, heads))) for head in range(1, heads, 2)
     ]
     project(groups[0])
-    for place, group in enumerate(groups):
-        if place + 1 < len(groups):
-            project(groups[place + 1])
+    attend(0)
+    send(0)
+    if heads > 1:
+        project(groups[1])
+    for place, group in enumerate(groups[1:], 1):
         for head in group:
+            if head == group[-1] and place + 1 < len(groups):
+                project(groups[place + 1])
             attend(head)
-
-        @pl.when(stage < last)
-        def _():
-            for head in group:
-                for copy in next_sends(head):
-                    copy.start()
-
-        @pl.when(stage == last)
-        def _():
-            for head in group:
-                for step in range(1, seq_count):
-                    out_copy(head, step).start()
-                out_own(head).start()
+            send(head)
 
     @pl.when(stage == 0)
     def _():
@@ -428,7 +443,7 @@
 
     @pl.when(stage > 0)
     def _():
-        back_copy(stage - 1).wait_send()
+        each_back(lambda place: back_copy(place, stage - 1).wait_send())
 
         def passed(head, carry):
             for copy in next_passes(head):
@@ -445,7 +460,7 @@
             return carry
 
         lax.fori_loop(0, heads, sent, 0)
-        back_copy(stage + 1).wait_recv()
+        each_back(lambda place: back_copy(place, stage + 1).wait_recv())
 
     @pl.when(stage == last)
     def _():
@@ -477,7 +492,7 @@
     dma = pltpu.SemaphoreType.DMA
     finished = pl.pallas_call(
         functools.partial(kernel, (patches, rows_dev, seq_count, pipe_count, heads)),
-        out_shape=jax.ShapeDtypeStruct((seq_count * heads, block, HEAD_DIM), bf16),
+        out_shape=jax.ShapeDtypeStruct((block, width), bf16),
         in_specs=[smem, smem, anywhere, anywhere, vmem, vmem, anywhere],
         out_specs=anywhere,
         scratch_shapes=[
@@ -502,14 +517,14 @@
             dma((heads, 2)),
             dma((heads, seq_count)),
             dma((heads, seq_count)),
-            dma(()),
-            dma(()),
+            dma((seq_count * heads,)),
+            dma((seq_count * heads,)),
         ],
         compiler_params=pltpu.CompilerParams(
             collective_id=0, has_side_effects=True, vmem_limit_bytes=56 * 1024 * 1024
         ),
     )(timestep, order, latent.reshape(block, width), weights, mods, tiles.T, stale)
-    return jnp.transpose(finished, (1, 0, 2)).reshape(1, patches, rows_dev, width)
+    return finished.reshape(1, patches, rows_dev, width)
 
 
 def solution(mesh):

time: 38.3 us -> 39.3 us (1.026)
  Pallas kernels: 35.4 us -> 36.7 us
  local copies, waits for them, and re-layouts: 2.12 us -> 1.72 us
    unnamed x0 -> x1, local copies, waits for them, and re-layouts: none -> 1.72 us
    pallas_call x1, Pallas kernels: 35.4 us -> 36.7 us  [local(): pl.pallas_call(functools.partial(kernel, (patches, rows_dev, seq_count, p...]
    transpose x1 -> x0, local copies, waits for them, and re-layouts: 1.2 us -> none  [local(): jnp.transpose(finished, (1, 0, 2)).reshape(1, patches, rows_dev, width)]
    reshape x1 -> x0, local copies, waits for them, and re-layouts: 0.92 us -> none  [local(): jnp.transpose(finished, (1, 0, 2)).reshape(1, patches, rows_dev, width)]
where the time goes in v6:
time: 39.3 us; the launch traced here: 39.1 us
  Pallas kernels  36.7 us (93%)
  local copies, waits for them, and re-layouts  1.72 us (4%)
  between operations  0.66 us (2%)
    pallas_call x1, Pallas kernels, local(): pl.pallas_call(functools.partial(kernel, (patches, rows_dev, seq_count, p...  36.7 us
    unnamed x1, local copies, waits for them, and re-layouts  1.72 us

profile of v6, /device:TPU:1, one launch (start us, length us, event | category | flops | bytes accessed | tf_op | source)
XLA Modules:
  0.0 39.1 jit_solution(11810138772790318679)
XLA Ops:
  0.7 36.7 %shard_map.73 = bf16[64,2560]{1,0:T(8,128)(2,1)} custom-call(s32[1]{0:T(128)S(6)} %copy.9.timestep_ref, s32[8]{0:T(128)} %order_ref.1, bf16[64,2560]{1,0:T(8,128)(2,1)} %bitcast.13, bf16[3,2560,640]{2,1,0:T(8,128)(2,1)} %bitcast.10, f32[3,8,2560]{2,1,0:T(8,128)} %bitcast.14, s32[6,16]{1,0:T(8,128)} %bitcast.15, bf16[256,2,640]{2,1,0:T(2,128)(2,1)} %bitcast.12), custom_call_target="tpu_custom_call" | custom-call | tf_op jit(solution)/shard_map/pallas_call | solution.py:493
  37.4 1.7 %copy.10 = bf16[1,8,8,2560]{3,2,1,0:T(8,128)(2,1)} copy(bf16[1,8,8,2560]{3,2,1,0:T(8,128)(2,1)} %bitcast.11) | data formatting | bytes 655360

commit v7 on v6

--- a/solution.py
+++ b/solution.py
@@ -58,6 +58,7 @@
     stage = lax.axis_index("pipe")
     me = lax.axis_index("seq")
     last = pipe_count - 1
+    helper = min(1, last)
     block = patches * rows_dev
     tokens = block * seq_count
     local_w = heads * HEAD_DIM
@@ -100,7 +101,7 @@
             dst_ref=arrived.at[half_of(me, half, block)],
             send_sem=lat_send.at[slot],
             recv_sem=lat_recv.at[me, half],
-            device_id={"seq": target},
+            device_id={"pipe": 0, "seq": target},
             device_id_type=MESH,
         )
 
@@ -115,13 +116,11 @@
             device_id_type=MESH,
         )
 
-    def latent_sends():
-        return (
-            latent_copy(0, 0, across_x),
-            latent_copy(1, 1, across_y),
-            latent_copy(2, 1, across_x),
-            latent_copy(3, 0, across_y),
-        )
+    def latent_sends_x():
+        return latent_copy(0, 0, across_x), latent_copy(2, 1, across_x)
+
+    def latent_sends_y():
+        return latent_copy(1, 1, across_y), latent_copy(3, 0, across_y)
 
     def latent_passes():
         return latent_pass(4, across_x, 0, across_y), latent_pass(5, across_y, 1, across_x)
@@ -239,7 +238,12 @@
 
     @pl.when(stage == 0)
     def _():
-        for copy in latent_sends():
+        for copy in latent_sends_x():
+            copy.start()
+
+    @pl.when(stage == helper)
+    def _():
+        for copy in latent_sends_y():
             copy.start()
 
     stale_copy().start()
@@ -393,17 +397,13 @@
         )
         fresh_p = jnp.exp2(fresh_s - largest)
         stale_p = jnp.exp2(stale_s - largest)
-        ones = jnp.ones((tokens, HEAD_DIM), jnp.bfloat16)
+        total = jnp.sum(fresh_p, axis=-1, keepdims=True) + jnp.sum(stale_p, axis=-1, keepdims=True)
         mixed = jnp.dot(
-            fresh_p.astype(jnp.bfloat16),
-            jnp.concatenate([qkv[head, 2], ones], axis=1),
-            preferred_element_type=jnp.float32,
+            fresh_p.astype(jnp.bfloat16), qkv[head, 2], preferred_element_type=jnp.float32
         ) + jnp.dot(
-            stale_p.astype(jnp.bfloat16),
-            jnp.concatenate([stale[1, :, lanes], ones], axis=1),
-            preferred_element_type=jnp.float32,
-        )
-        attended = (mixed[:, :HEAD_DIM] / mixed[:, HEAD_DIM:]).astype(jnp.bfloat16).astype(jnp.float32)
+            stale_p.astype(jnp.bfloat16), stale[1, :, lanes], preferred_element_type=jnp.float32
+        )
+        attended = (mixed / total).astype(jnp.bfloat16).astype(jnp.float32)
         mine = columns_of(me, head)
         result[head] = (
             hidden[place_of(me, head)].astype(jnp.float32) + mods[2:3, mine] * attended
@@ -421,24 +421,24 @@
                 out_copy(head, step).start()
             out_own(head).start()
 
-    groups = [(0,)] + [
-        tuple(range(head, min(head + 2, heads))) for head in range(1, heads, 2)
-    ]
+    groups = [tuple(range(head, min(head + 2, heads))) for head in range(0, heads, 2)]
     project(groups[0])
-    attend(0)
-    send(0)
-    if heads > 1:
-        project(groups[1])
-    for place, group in enumerate(groups[1:], 1):
+    for place, group in enumerate(groups):
+        if place + 1 < len(groups):
+            project(groups[place + 1])
         for head in group:
-            if head == group[-1] and place + 1 < len(groups):
-                project(groups[place + 1])
             attend(head)
+        for head in group:
             send(head)
 
     @pl.when(stage == 0)
     def _():
-        for copy in latent_sends() + latent_passes():
+        for copy in latent_sends_x() + latent_passes():
+            copy.wait_send()
+
+    @pl.when(stage == helper)
+    def _():
+        for copy in latent_sends_y():
             copy.wait_send()
 
     @pl.when(stage > 0)

time: 39.3 us -> 38.5 us (0.980)
  Pallas kernels: 36.7 us -> 35.9 us
    pallas_call x1, Pallas kernels: 36.7 us -> 35.9 us  [local(): pl.pallas_call(functools.partial(kernel, (patches, rows_dev, seq_count, p...]
where the time goes in v7:
time: 38.5 us; the launch traced here: 38.3 us
  Pallas kernels  35.9 us (93%)
  local copies, waits for them, and re-layouts  1.72 us (4%)
  between operations  0.66 us (2%)
    pallas_call x1, Pallas kernels, local(): pl.pallas_call(functools.partial(kernel, (patches, rows_dev, seq_count, p...  35.9 us
    unnamed x1, local copies, waits for them, and re-layouts  1.72 us

profile of v7, /device:TPU:1, one launch (start us, length us, event | category | flops | bytes accessed | tf_op | source)
XLA Modules:
  0.0 38.3 jit_solution(6392635390002847352)
XLA Ops:
  0.7 35.9 %shard_map.73 = bf16[64,2560]{1,0:T(8,128)(2,1)} custom-call(s32[1]{0:T(128)S(6)} %copy.9.timestep_ref, s32[8]{0:T(128)} %order_ref.1, bf16[64,2560]{1,0:T(8,128)(2,1)} %bitcast.13, bf16[3,2560,640]{2,1,0:T(8,128)(2,1)} %bitcast.10, f32[3,8,2560]{2,1,0:T(8,128)} %bitcast.14, s32[6,16]{1,0:T(8,128)} %bitcast.15, bf16[256,2,640]{2,1,0:T(2,128)(2,1)} %bitcast.12), custom_call_target="tpu_custom_call" | custom-call | tf_op jit(solution)/shard_map/pallas_call | solution.py:493
  36.6 1.7 %copy.10 = bf16[1,8,8,2560]{3,2,1,0:T(8,128)(2,1)} copy(bf16[1,8,8,2560]{3,2,1,0:T(8,128)(2,1)} %bitcast.11) | data formatting | bytes 655360

commit v8 on v7

--- a/solution.py
+++ b/solution.py
@@ -53,6 +53,8 @@
     out_recv,
     back_send,
     back_recv,
+    modulation,
+    mods_sem,
 ):
     patches, rows_dev, seq_count, pipe_count, heads = sizes
     stage = lax.axis_index("pipe")
@@ -163,22 +165,18 @@
             next_pass(head, 1, across_y, 1, across_x),
         )
 
-    def back_copy(place, target):
-        return pltpu.make_async_remote_copy(
-            src_ref=hidden.at[place, rows_of(me)],
-            dst_ref=out_ref.at[:, columns_of(0, place)],
-            send_sem=back_send.at[place],
-            recv_sem=back_recv.at[place],
+    def back_copy(target):
+        return pltpu.make_async_remote_copy(
+            src_ref=arrived.at[rows_of(me)],
+            dst_ref=out_ref,
+            send_sem=back_send,
+            recv_sem=back_recv,
             device_id={"pipe": target},
             device_id_type=MESH,
         )
 
-    def each_back(act):
-        def one(place, carry):
-            act(place)
-            return carry
-
-        lax.fori_loop(0, columns, one, 0)
+    def mods_copy():
+        return pltpu.make_async_copy(modulation_ref, modulation, mods_sem)
 
     def out_copy(head, step):
         return pltpu.make_async_remote_copy(
@@ -224,6 +222,8 @@
             pl.semaphore_signal(
                 barrier, inc=1, device_id={"pipe": stage + 1, "seq": peer(step)}, device_id_type=MESH
             )
+
+    mods_copy().start()
 
     @pl.when(stage == 0)
     def _():
@@ -250,9 +250,10 @@
     for part in range(3):
         weight_copy(part).start()
 
-    picked_step = lax.broadcasted_iota(jnp.int32, modulation_ref.shape[1:], 0) == timestep_ref[0]
+    mods_copy().wait()
+    picked_step = lax.broadcasted_iota(jnp.int32, modulation.shape[1:], 0) == timestep_ref[0]
     for part in range(3):
-        row = jnp.sum(jnp.where(picked_step, modulation_ref[part], 0.0), axis=0, keepdims=True)
+        row = jnp.sum(jnp.where(picked_step, modulation[part], 0.0), axis=0, keepdims=True)
         mods[pl.ds(part, 1), :] = row + 1.0 if part == 1 else row
 
     def normalize_rows(rows, block_rows):
@@ -338,7 +339,6 @@
 
         lax.fori_loop(0, heads, pass_on, 0)
         lax.fori_loop(0, heads, arrive, 0)
-        each_back(lambda place: back_copy(place, stage - 1).start())
 
     @pl.when(stage == 0)
     def _():
@@ -361,6 +361,11 @@
             return carry
 
         lax.fori_loop(0, seq_count, normalize_block, 0)
+        for rows in row_chunks(me):
+            arrived[rows, :] = jnp.concatenate(
+                [hidden[place, rows, :] for place in range(columns)], axis=1
+            )
+        back_copy(stage - 1).start()
 
     for part in range(3):
         weight_copy(part).wait()
@@ -443,7 +448,7 @@
 
     @pl.when(stage > 0)
     def _():
-        each_back(lambda place: back_copy(place, stage - 1).wait_send())
+        back_copy(stage - 1).wait_send()
 
         def passed(head, carry):
             for copy in next_passes(head):
@@ -460,7 +465,7 @@
             return carry
 
         lax.fori_loop(0, heads, sent, 0)
-        each_back(lambda place: back_copy(place, stage + 1).wait_recv())
+        back_copy(stage + 1).wait_recv()
 
     @pl.when(stage == last)
     def _():
@@ -493,7 +498,7 @@
     finished = pl.pallas_call(
         functools.partial(kernel, (patches, rows_dev, seq_count, pipe_count, heads)),
         out_shape=jax.ShapeDtypeStruct((block, width), bf16),
-        in_specs=[smem, smem, anywhere, anywhere, vmem, vmem, anywhere],
+        in_specs=[smem, smem, anywhere, anywhere, anywhere, vmem, anywhere],
         out_specs=anywhere,
         scratch_shapes=[
             pltpu.VMEM((tokens, width), bf16),
@@ -517,8 +522,10 @@
             dma((heads, 2)),
             dma((heads, seq_count)),
             dma((heads, seq_count)),
-            dma((seq_count * heads,)),
-            dma((seq_count * heads,)),
+            dma(()),
+            dma(()),
+            pltpu.VMEM(mods.shape, jnp.float32),
+            dma(()),
         ],
         compiler_params=pltpu.CompilerParams(
             collective_id=0, has_side_effects=True, vmem_limit_bytes=56 * 1024 * 1024

time: 38.5 us -> 37.9 us (0.984)
  Pallas kernels: 35.9 us -> 35.3 us
    pallas_call x1, Pallas kernels: 35.9 us -> 35.3 us  [local(): pl.pallas_call(functools.partial(kernel, (patches, rows_dev, seq_count, p...]
where the time goes in v8:
time: 37.9 us; the launch traced here: 37.7 us
  Pallas kernels  35.3 us (93%)
  local copies, waits for them, and re-layouts  1.72 us (5%)
  between operations  0.66 us (2%)
    pallas_call x1, Pallas kernels, local(): pl.pallas_call(functools.partial(kernel, (patches, rows_dev, seq_count, p...  35.3 us
    unnamed x1, local copies, waits for them, and re-layouts  1.72 us

profile of v8, /device:TPU:1, one launch (start us, length us, event | category | flops | bytes accessed | tf_op | source)
XLA Modules:
  0.0 37.7 jit_solution(14142470087052688230)
XLA Ops:
  0.7 35.3 %shard_map.73 = bf16[64,2560]{1,0:T(8,128)(2,1)} custom-call(s32[1]{0:T(128)S(6)} %copy.9.timestep_ref, s32[8]{0:T(128)} %order_ref.1, bf16[64,2560]{1,0:T(8,128)(2,1)} %bitcast.13, bf16[3,2560,640]{2,1,0:T(8,128)(2,1)} %bitcast.10, f32[3,8,2560]{2,1,0:T(8,128)} %bitcast.14, s32[6,16]{1,0:T(8,128)} %bitcast.15, bf16[256,2,640]{2,1,0:T(2,128)(2,1)} %bitcast.12), custom_call_target="tpu_custom_call" | custom-call | tf_op jit(solution)/shard_map/pallas_call | solution.py:498
  36.0 1.7 %copy.10 = bf16[1,8,8,2560]{3,2,1,0:T(8,128)(2,1)} copy(bf16[1,8,8,2560]{3,2,1,0:T(8,128)(2,1)} %bitcast.11) | data formatting | bytes 655360

commit v9 on v8

--- a/solution.py
+++ b/solution.py
@@ -426,7 +426,9 @@
                 out_copy(head, step).start()
             out_own(head).start()
 
-    groups = [tuple(range(head, min(head + 2, heads))) for head in range(0, heads, 2)]
+    groups = [(0,)] + [
+        tuple(range(head, min(head + 2, heads))) for head in range(1, heads, 2)
+    ]
     project(groups[0])
     for place, group in enumerate(groups):
         if place + 1 < len(groups):

time: 37.9 us -> 37.8 us (level)
  no operation moved by 1% of the time
where the time goes in v9:
time: 37.8 us; the launch traced here: 37.6 us
  Pallas kernels  35.2 us (93%)
  local copies, waits for them, and re-layouts  1.72 us (5%)
  between operations  0.66 us (2%)
    pallas_call x1, Pallas kernels, local(): pl.pallas_call(functools.partial(kernel, (patches, rows_dev, seq_count, p...  35.2 us
    unnamed x1, local copies, waits for them, and re-layouts  1.72 us

profile of v9, /device:TPU:1, one launch (start us, length us, event | category | flops | bytes accessed | tf_op | source)
XLA Modules:
  0.0 37.6 jit_solution(16277045542270313699)
XLA Ops:
  0.7 35.2 %shard_map.73 = bf16[64,2560]{1,0:T(8,128)(2,1)} custom-call(s32[1]{0:T(128)S(6)} %copy.9.timestep_ref, s32[8]{0:T(128)} %order_ref.1, bf16[64,2560]{1,0:T(8,128)(2,1)} %bitcast.13, bf16[3,2560,640]{2,1,0:T(8,128)(2,1)} %bitcast.10, f32[3,8,2560]{2,1,0:T(8,128)} %bitcast.14, s32[6,16]{1,0:T(8,128)} %bitcast.15, bf16[256,2,640]{2,1,0:T(2,128)(2,1)} %bitcast.12), custom_call_target="tpu_custom_call" | custom-call | tf_op jit(solution)/shard_map/pallas_call | solution.py:500
  35.9 1.7 %copy.10 = bf16[1,8,8,2560]{3,2,1,0:T(8,128)(2,1)} copy(bf16[1,8,8,2560]{3,2,1,0:T(8,128)(2,1)} %bitcast.11) | data formatting | bytes 655360
